TPU v7x, 32 devices: a whole 2x2x4 slice. The times are simulated.
32 devices in a mesh: row: 8 (over y, x, core), col: 4 (over z).
Axes of the slice: x: 2, y: 2, z: 4, core: 2. Of those that a mesh axis runs over, the one named last changes fastest.
Arguments:
- k_vals: float32 [128, 15, 64, 64], P('row'), may hold values from -0.1875 to 0.1875
- k_cols: int32 [128, 15], P('row'), may hold values from -8 to 135, as said below
- p_vals: float32 [128, 3, 64, 64], P('row', None, None, 'col'), may hold values from -1.2 to 1.2
- p_cols: int32 [128, 3], P('row'), may hold values from -1 to 15, as said below
Outputs:
- coarse: float32 [16, 7, 64, 64], P('row', None, None, 'col')
Inputs may be any that keep to these rules, and one draw needn't show every extreme that they name: Each k_cols[i, s] - i lies between -8 and 8; within a block row the columns differ; a column outside 0 to 127 stands for an absent block. Each p_cols[k, s] is -1 for an absent block or lies within 1 of k // 8, the aggregate of block row k; the present columns of a row differ, and the aggregate of every block row is present.
All inputs are finite; a program needn't handle non-finite values.
Results may differ from a plain program's by a relative error of at most 0.0001.
Values sent between devices are 32-bit elements; how exact they have to be, the bound alone decides.
No kernel may reach another device: no remote copies, remote signals or barrier semaphores. Data moves between devices by JAX's collectives and lax.ppermute only.
A program may use at most 128 MiB of HBM per device.

v0:
```python
import jax
import jax.numpy as jnp
from jax import lax
from jax.sharding import PartitionSpec as P

AGG = 8


def extended_2(cells, sides, width):
    for axis, dim in sides:
        count = lax.axis_size(axis)
        ends = count - 1
        head = lax.slice_in_dim(cells, 0, width, axis=dim)
        tail = lax.slice_in_dim(cells, cells.shape[dim] - width, cells.shape[dim], axis=dim)
        cells = jnp.concatenate(
            [
                lax.ppermute(tail, axis, [(i, (i + 1) % count) for i in range(ends)]),
                cells,
                lax.ppermute(head, axis, [((i + 1) % count, i) for i in range(ends)]),
            ],
            axis=dim,
        )
    return cells


def place_window(p_vals, p_cols, aggregate, blocks_all):
    present = (p_cols >= 0) & (p_cols < blocks_all)
    position = p_cols - aggregate[:, None] + 1
    selector = (
        (position[:, :, None] == jnp.arange(3, dtype=jnp.int32)[None, None, :])
        & present[:, :, None]
    ).astype(jnp.float32)
    return jnp.einsum("jtu,jtbc->jubc", selector, p_vals, precision=lax.Precision.HIGHEST)


def stiff_rows(blocks, columns, first_row, padded, margin, total_rows):
    count = blocks.shape[0]
    fine_width = blocks.shape[2]
    share = padded.shape[3]
    aggregate = (first_row + jnp.arange(count, dtype=jnp.int32)) // AGG
    in_range = (columns >= 0) & (columns < total_rows)
    safe_cols = jnp.clip(columns, 0, total_rows - 1)
    near_agg = safe_cols // AGG - aggregate[:, None] + 1
    side_mask = (
        (near_agg[:, :, None] == jnp.arange(3, dtype=jnp.int32)[None, None, :])
        & in_range[:, :, None]
    ).astype(jnp.float32)
    local_cols = jnp.clip(columns - first_row + margin, 0, padded.shape[0] - 1)
    picked = jnp.take(padded, local_cols, axis=0)
    product = jnp.einsum("isab,isubc->isuac", blocks, picked, precision=lax.Precision.HIGHEST)
    mixed_terms = jnp.einsum(
        "ise,isuac->ieuac", side_mask, product, precision=lax.Precision.HIGHEST
    )
    result = jnp.zeros((count, 5, fine_width, share), jnp.float32)
    for offset in range(3):
        result = result.at[:, offset : offset + 3].add(mixed_terms[:, offset])
    return result


def make_partial(stiff_prolong, column_piece):
    count = stiff_prolong.shape[0]
    groups = count // AGG
    share = stiff_prolong.shape[3]
    upper_side = stiff_prolong.reshape(groups, AGG, 5, stiff_prolong.shape[2], share)
    lower_side = column_piece.reshape(groups, AGG, 3, column_piece.shape[2], column_piece.shape[3])
    grouped = jnp.einsum(
        "giubc,giwbd->guwcd", lower_side, upper_side, precision=lax.Precision.HIGHEST
    )
    partial_value = jnp.zeros((groups + 2, 7, column_piece.shape[3], share), jnp.float32)
    for left_slot in range(3):
        for right_slot in range(5):
            partial_value = partial_value.at[
                left_slot : left_slot + groups, right_slot - left_slot + 2
            ].add(grouped[:, left_slot, right_slot])
    return partial_value


def body(k_vals, k_cols, p_vals, p_cols):
    own_rows = k_vals.shape[0]
    groups = own_rows // AGG
    total_rows = own_rows * lax.axis_size("row")
    blocks_all = total_rows // AGG
    first_row = lax.axis_index("row") * own_rows
    aggregate = (first_row + jnp.arange(own_rows, dtype=jnp.int32)) // AGG
    window = place_window(p_vals, p_cols, aggregate, blocks_all)
    extended = extended_2(window, (("row", 0),), AGG)
    stiff_prolong = stiff_rows(k_vals, k_cols, first_row, extended, AGG, total_rows)
    terms = make_partial(stiff_prolong, lax.all_gather(window, "col", axis=3, tiled=True))
    bordered = extended_2(terms, (("row", 0),), 1)
    coarse = terms[1 : groups + 1]
    coarse = coarse.at[0].add(bordered[0])
    coarse = coarse.at[groups - 1].add(bordered[groups + 3])
    return coarse


def solution(mesh):
    placed = (
        P("row", None, None, None),
        P("row", None),
        P("row", None, None, "col"),
        P("row", None),
    )
    return jax.shard_map(
        body, mesh=mesh, in_specs=placed, out_specs=P("row", None, None, "col"), check_vma=False
    )
```

profile of v0, /device:TPU:27, one launch (start us, length us, event | category | flops | bytes accessed | tf_op | source)
XLA Modules:
  0.0 113.9 jit_solution(8415049966623661635)
XLA Ops:
  0.0 0.0 copy-start
  0.0 0.7 compare_and_fusion.2
  0.8 0.7 subtract_add_fusion
  1.4 0.1 copy.5
  1.5 0.1 copy.6
  1.6 0.0 copy-done
  1.6 0.7 fusion.12
  2.3 0.1 fusion.59
  2.5 3.7 %collective-permute-start = (f32[8,3,64,16]{2,1,3,0:T(4,128)S(1)}, f32[8,3,64,16]{2,1,3,0:T(4,128)S(1)}, u32[]{:S(2)}, u32[]{:S(2)}) collective-permute-start(f32[8,3,64,16]{2,1,3,0:T(4,128)S(1)} %get-tuple-element.254), channel_id=1, source_target_pairs={{0,4},{4,8},{8,12},{12,16},{16,20},{20,24},{24,28},{1,5},{5,9},{9,... | collective-permute-start | bytes 294920 | tf_op jit(solution)/shard_map/ppermute | solution.py:17
  6.2 1.9 %collective-permute-start.1 = (f32[8,3,64,16]{2,1,3,0:T(4,128)S(1)}, f32[8,3,64,16]{2,1,3,0:T(4,128)S(1)}, u32[]{:S(2)}, u32[]{:S(2)}) collective-permute-start(f32[8,3,64,16]{2,1,3,0:T(4,128)S(1)} %get-tuple-element.255), channel_id=1, source_target_pairs={{4,0},{8,4},{12,8},{16,12},{20,16},{24,20},{28,24},{5,1},{9,5},{13... | collective-permute-start | bytes 294920 | tf_op jit(solution)/shard_map/ppermute | solution.py:19
  8.1 0.7 compare_and_fusion
  8.8 0.8 fusion.56
  9.6 37.5 %all_gather.3 = f32[16,3,64,64]{2,1,3,0:T(4,128)} all-gather(f32[16,3,64,16]{2,1,3,0:T(4,128)S(1)} %fusion.12), channel_id=1, replica_groups=mesh['row'=8,'col'=4] {'col'}, dimensions={3}, use_global_device_ids=true | all-gather | bytes 983040 | tf_op jit(solution)/shard_map/all_gather | solution.py:88
  47.1 0.6 fusion.65
  47.7 0.6 fusion.64
  48.3 0.6 fusion.63
  48.8 0.6 fusion.62
  49.5 1.4 %and_reduce_fusion.4 = pred[]{:T(512)} fusion(s32[4]{0:T(128)} %constant.605.clone.1, s32[1]{0:T(128)} %constant.604.clone.1, s32[2]{0:T(128)S(1)} %iota_multiply_fusion.4), kind=kLoop, calls=%fused_computation.98 | loop fusion | flops 23 | bytes 29 | tf_op jit(solution)/shard_map/reduce.23
  50.9 1.5 %and_reduce_fusion = (pred[]{:T(512)}, pred[]{:T(512)}, pred[]{:T(512)}, pred[]{:T(512)}) fusion(s32[4]{0:T(128)} %constant.605.clone.1, s32[1]{0:T(128)} %constant.604.clone.1, s32[2]{0:T(128)S(1)} %get-tuple-element.271, s32[2]{0:T(128)S(1)} %get-tuple-element.272, s32[2]{0:T(128)S(1)} %get-tuple-element.274, s32[2]{0:T(128)S(1)} %get-tuple-element.273), kind=kLoop, calls=%fused_computation.92 | loop fusion | flops 92 | bytes 56 | tf_op jit(solution)/shard_map/reduce.27
  52.4 0.6 fusion.61
  53.0 0.1 reshape.885
  53.1 0.0 collective-permute-done
  53.1 0.0 collective-permute-done.1
  53.1 0.4 pad_maximum_fusion
  53.5 11.7 %gather_fusion = f32[240,3,64,16]{2,1,3,0:T(4,128)} fusion(f32[32,3,64,16]{2,1,3,0:T(4,128)S(1)} %pad_maximum_fusion, s32[1024]{0:T(1024)S(1)} %pad_clamp_fusion), kind=kCustom, calls=%fused_computation | custom fusion | bytes 5899200 | tf_op jit(solution)/shard_map/jit(_take)/gather | solution.py:49
  65.3 5.0 %broadcast_select_fusion = f32[16,15,3,64,16]{3,2,4,1,0:T(4,128)S(1)} fusion(f32[16,15,3,64,16]{3,2,4,1,0:T(4,128)} %bitcast.161, pred[16,15]{1,0:T(8,128)(4,1)S(1)} %get-tuple-element.249), kind=kLoop, calls=%fused_computation.7 | loop fusion | flops 737280 | bytes 5898480 | tf_op jit(solution)/shard_map/jit(_take)/select_n | solution.py:49
  70.3 15.0 %fusion = f32[16,15,3,16,64]{4,3,2,1,0:T(8,128)S(1)} fusion(f32[16,15,64,64]{3,2,1,0:T(8,128)} %param.44, f32[16,15,3,64,16]{3,2,4,1,0:T(4,128)S(1)} %broadcast_select_fusion), kind=kOutput, calls=%fused_computation.1 | convolution fusion | flops 566231040 | bytes 9830400 | tf_op jit(solution)/shard_map/isab,isubc->isuac/dot_general | solution.py:50
  85.3 0.0 copy-start.1
  85.3 4.0 %fusion.2 = f32[16,3,3,64,16]{3,1,4,2,0:T(4,128)S(1)} fusion(f32[16,15,3,16,64]{4,3,2,1,0:T(8,128)S(1)} %fusion, s32[16,15]{1,0:T(8,128)S(1)} %fusion.56, pred[16,15]{1,0:T(8,128)(4,1)S(1)} %get-tuple-element.258), kind=kOutput, calls=%fused_computation.3 | convolution fusion | flops 26543520 | bytes 3540144 | tf_op jit(solution)/shard_map/ise,isuac->ieuac/dot_general | solution.py:51
  89.3 0.8 fusion.58
  90.2 0.1 add_dynamic-update-slice_fusion
  90.3 0.1 fusion.14
  90.4 0.0 copy-done.1
  90.4 2.0 %fusion.8 = f32[2,3,5,64,16]{3,4,1,2,0:T(8,128)S(1)} fusion(f32[2,8,3,64,64,1]{3,2,4,1,0,5:T(4,128)S(1)} %bitcast.163, f32[2,8,5,64,16,1]{3,4,2,1,0,5:T(8,128)S(1)} %bitcast.162), kind=kOutput, calls=%fused_computation.10 | convolution fusion | flops 188743680 | bytes 1236992 | tf_op jit(solution)/shard_map/giubc,giwbd->guwcd/dot_general | solution.py:66
  92.4 1.9 %fusion.49 = f32[4,7,64,16]{2,3,0,1:T(8,128)S(1)} fusion(f32[4,7,64,16]{2,3,0,1:T(8,128)S(1)} %broadcast_in_dim.11, s32[]{:T(128)} %bitcast.19, s32[]{:T(128)} %bitcast.20, f32[2,3,5,64,16]{3,4,1,2,0:T(8,128)S(1)} %fusion.8, pred[]{:T(512)} %and_reduce_fusion.4), kind=kLoop, calls=%fused_computation.74 | loop fusion | flops 2048 | bytes 32777 | tf_op jit(solution)/shard_map/scatter-add | solution.py:74
  94.3 1.8 %fusion.23 = f32[4,7,64,16]{2,3,0,1:T(8,128)S(1)} fusion(f32[4,7,64,16]{2,3,0,1:T(8,128)S(1)} %fusion.49, s32[]{:T(128)} %bitcast.21, s32[]{:T(128)} %bitcast.22, f32[2,3,5,64,16]{3,4,1,2,0:T(8,128)S(1)} %fusion.8, pred[]{:T(512)} %get-tuple-element.261), kind=kLoop, calls=%fused_computation.33 | loop fusion | flops 4096 | bytes 49161 | tf_op jit(solution)/shard_map/scatter-add | solution.py:74
  96.1 1.9 %fusion.24 = f32[4,7,64,16]{2,3,0,1:T(8,128)S(1)} fusion(f32[4,7,64,16]{2,3,0,1:T(8,128)S(1)} %fusion.23, s32[]{:T(128)} %bitcast.25, s32[]{:T(128)} %bitcast.26, f32[2,3,5,64,16]{3,4,1,2,0:T(8,128)S(1)} %fusion.8, pred[]{:T(512)} %get-tuple-element.262), kind=kLoop, calls=%fused_computation.34 | loop fusion | flops 4096 | bytes 49161 | tf_op jit(solution)/shard_map/scatter-add | solution.py:74
  98.0 1.9 %fusion.25 = f32[4,7,64,16]{2,3,0,1:T(8,128)S(1)} fusion(f32[4,7,64,16]{2,3,0,1:T(8,128)S(1)} %fusion.24, s32[]{:T(128)} %bitcast.28, s32[]{:T(128)} %bitcast.29, f32[2,3,5,64,16]{3,4,1,2,0:T(8,128)S(1)} %fusion.8, pred[]{:T(512)} %get-tuple-element.246), kind=kLoop, calls=%fused_computation.35 | loop fusion | flops 4096 | bytes 49161 | tf_op jit(solution)/shard_map/scatter-add | solution.py:74
  100.0 1.9 %fusion.26 = f32[4,7,64,16]{2,3,0,1:T(8,128)S(1)} fusion(f32[4,7,64,16]{2,3,0,1:T(8,128)S(1)} %fusion.25, s32[]{:T(128)} %bitcast.31, s32[]{:T(128)} %bitcast.32, f32[2,3,5,64,16]{3,4,1,2,0:T(8,128)S(1)} %fusion.8, pred[]{:T(512)} %get-tuple-element.245), kind=kLoop, calls=%fused_computation.36 | loop fusion | flops 4096 | bytes 49161 | tf_op jit(solution)/shard_map/scatter-add | solution.py:74
  102.0 4.8 %collective-permute-start.2 = (f32[1,7,64,16]{2,3,0,1:T(8,128)S(1)}, f32[1,7,64,16]{2,3,0,1:T(8,128)S(1)}, u32[]{:S(2)}, u32[]{:S(2)}) collective-permute-start(f32[1,7,64,16]{2,3,0,1:T(8,128)S(1)} %get-tuple-element.257), channel_id=1, source_target_pairs={{0,4},{4,8},{8,12},{12,16},{16,20},{20,24},{24,28},{1,5},{5,9},{9,... | collective-permute-start | bytes 86024 | tf_op jit(solution)/shard_map/ppermute | solution.py:17
  106.9 1.9 %collective-permute-start.3 = (f32[1,7,64,16]{2,3,0,1:T(8,128)S(1)}, f32[1,7,64,16]{2,3,0,1:T(8,128)S(1)}, u32[]{:S(2)}, u32[]{:S(2)}) collective-permute-start(f32[1,7,64,16]{2,3,0,1:T(8,128)S(1)} %get-tuple-element.256), channel_id=1, source_target_pairs={{4,0},{8,4},{12,8},{16,12},{20,16},{24,20},{28,24},{5,1},{9,5},{13... | collective-permute-start | bytes 86024 | tf_op jit(solution)/shard_map/ppermute | solution.py:19
  108.8 0.0 collective-permute-done.2
  108.8 4.4 %collective-permute-done.3 = f32[1,7,64,16]{2,3,0,1:T(8,128)S(1)} collective-permute-done((f32[1,7,64,16]{2,3,0,1:T(8,128)S(1)}, f32[1,7,64,16]{2,3,0,1:T(8,128)S(1)}, u32[]{:S(2)}, u32[]{:S(2)}) %collective-permute-start.3) | collective-permute-done | bytes 28704 | tf_op jit(solution)/shard_map/ppermute | solution.py:19
  113.3 0.7 copy.26
  (21 shorter events, 0.2 us)
Async XLA Ops:
  0.0 1.6 %copy-start = (f32[16,3,64,16]{2,3,1,0:T(8,128)S(1)}, f32[16,3,64,16]{2,3,1,0:T(8,128)}, u32[]{:S(2)}) copy-start(f32[16,3,64,16]{2,3,1,0:T(8,128)} %param.46) | copy-start | bytes 589828
  2.5 50.6 %collective-permute-start = (f32[8,3,64,16]{2,1,3,0:T(4,128)S(1)}, f32[8,3,64,16]{2,1,3,0:T(4,128)S(1)}, u32[]{:S(2)}, u32[]{:S(2)}) collective-permute-start(f32[8,3,64,16]{2,1,3,0:T(4,128)S(1)} %get-tuple-element.254), channel_id=1, source_target_pairs={{0,4},{4,8},{8,12},{12,16},{16,20},{20,24},{24,28},{1,5},{5,9},{9,... | collective-permute-start | bytes 294920 | tf_op jit(solution)/shard_map/ppermute | solution.py:17
  6.2 47.0 %collective-permute-start.1 = (f32[8,3,64,16]{2,1,3,0:T(4,128)S(1)}, f32[8,3,64,16]{2,1,3,0:T(4,128)S(1)}, u32[]{:S(2)}, u32[]{:S(2)}) collective-permute-start(f32[8,3,64,16]{2,1,3,0:T(4,128)S(1)} %get-tuple-element.255), channel_id=1, source_target_pairs={{4,0},{8,4},{12,8},{16,12},{20,16},{24,20},{28,24},{5,1},{9,5},{13... | collective-permute-start | bytes 294920 | tf_op jit(solution)/shard_map/ppermute | solution.py:19
  85.3 5.1 %copy-start.1 = (f32[16,3,64,64]{2,1,3,0:T(4,128)S(1)}, f32[16,3,64,64]{2,1,3,0:T(4,128)}, u32[]{:S(2)}) copy-start(f32[16,3,64,64]{2,1,3,0:T(4,128)} %all_gather.3) | copy-start | bytes 2359300
  102.0 6.8 %collective-permute-start.2 = (f32[1,7,64,16]{2,3,0,1:T(8,128)S(1)}, f32[1,7,64,16]{2,3,0,1:T(8,128)S(1)}, u32[]{:S(2)}, u32[]{:S(2)}) collective-permute-start(f32[1,7,64,16]{2,3,0,1:T(8,128)S(1)} %get-tuple-element.257), channel_id=1, source_target_pairs={{0,4},{4,8},{8,12},{12,16},{16,20},{20,24},{24,28},{1,5},{5,9},{9,... | collective-permute-start | bytes 86024 | tf_op jit(solution)/shard_map/ppermute | solution.py:17
  106.9 6.4 %collective-permute-start.3 = (f32[1,7,64,16]{2,3,0,1:T(8,128)S(1)}, f32[1,7,64,16]{2,3,0,1:T(8,128)S(1)}, u32[]{:S(2)}, u32[]{:S(2)}) collective-permute-start(f32[1,7,64,16]{2,3,0,1:T(8,128)S(1)} %get-tuple-element.256), channel_id=1, source_target_pairs={{4,0},{8,4},{12,8},{16,12},{20,16},{24,20},{28,24},{5,1},{9,5},{13... | collective-permute-start | bytes 86024 | tf_op jit(solution)/shard_map/ppermute | solution.py:19
where the time goes:
time: 114 us
  blocking collectives  37.5 us (33%)
  matrix products  21.6 us (19%)
  other arithmetic  21 us (18%)
  local copies, waits for them, and re-layouts  16.7 us (15%)
  starting transfers between devices  12.3 us (11%)
  waiting for transfers between devices  4.45 us (4%)
    all_gather x1, blocking collectives, body(): lax.all_gather(window, 'col', axis=3, tiled=True)  37.5 us
    dot_general x1, matrix products, stiff_rows(): jnp.einsum('isab,isubc->isuac', blocks, picked, precision=lax.Precision.H...  15 us
    gather x1, local copies, waits for them, and re-layouts, stiff_rows(): picked = jnp.take(padded, local_cols, axis=0)  11.7 us
    scatter-add x15, other arithmetic, make_partial(): partial_value = partial_value.at[left_slot:left_slot + groups, right_slot...  9.51 us
    ppermute x2, starting transfers between devices, extended_2(): lax.ppermute(tail, axis, [(i, (i + 1) % count) for i in range(ends)])  8.49 us
    select_n x1, other arithmetic, stiff_rows(): picked = jnp.take(padded, local_cols, axis=0)  5.04 us
    ppermute x2, waiting for transfers between devices, extended_2(): lax.ppermute(head, axis, [((i + 1) % count, i) for i in range(ends)])  4.44 us
    dot_general x1, matrix products, stiff_rows(): jnp.einsum('ise,isuac->ieuac', side_mask, product, precision=lax.Precisio...  4 us
  transfers between devices with their start and end apart: 4, of which 1 were waited for; matrix products, arithmetic and copies ran while one was open for 7% of the time, Pallas kernels for 0%

commit v1 on v0

v1 whole, which is shorter than its diff:
```python
import functools

import jax
import jax.numpy as jnp
from jax import lax
from jax.experimental import pallas as pl
from jax.experimental.pallas import tpu as pltpu
from jax.sharding import PartitionSpec as P

AGG = 8
PAIRS = AGG // 2


def split_high_low(value):
    high = value.astype(jnp.bfloat16)
    low = (value - high.astype(jnp.float32)).astype(jnp.bfloat16)
    return high, low


def pack_kernel(
    blocks_all, cols_hbm, p_hbm, both_ref, mine_ref, other_ref, mine_again, other_again,
    cols_ref, p_ref, sems,
):
    cols_copy = pltpu.make_async_copy(cols_hbm, cols_ref, sems.at[0])
    p_copy = pltpu.make_async_copy(p_hbm, p_ref, sems.at[1])
    cols_copy.start()
    p_copy.start()
    half = lax.axis_index("col") % 2
    first_agg = lax.axis_index("row") * 2
    blank = jnp.zeros(p_ref.shape[2:], jnp.float32)
    cols_copy.wait()
    p_copy.wait()
    for part, out_ref, again in ((0, mine_ref, mine_again), (1, other_ref, other_again)):
        group = half if part == 0 else 1 - half
        targets = []
        for window in range(3):
            target = first_agg + group - 1 + window
            targets.append(jnp.where((target >= 0) & (target < blocks_all), target, -2))
        for pair in range(PAIRS):
            rows = []
            for sub in range(2):
                row = group * AGG + 2 * pair + sub
                rows.append([(cols_ref[slot, row], p_ref[row, slot]) for slot in range(3)])
            for window, target in enumerate(targets):
                halves = []
                for slots in rows:
                    value = blank
                    for column, block in slots:
                        value = jnp.where(column == target, block, value)
                    halves.append(value)
                packed = jnp.concatenate(halves, axis=1)
                out_ref[pair, window] = packed
                again[pair, window] = packed
                both_ref[part * PAIRS + pair, window] = packed


def split_kernel(slots, total_rows, cols_hbm, k_hbm, out_ref, cols_ref, k_ref, cols_sem, sems):
    half = lax.axis_index("col") % 2
    first_row = lax.axis_index("row") * (2 * AGG) + half * AGG
    absent = 3 * AGG

    def k_copy(row):
        return pltpu.make_async_copy(k_hbm.at[half * AGG + row], k_ref.at[row], sems.at[row])

    cols_copy = pltpu.make_async_copy(cols_hbm, cols_ref, cols_sem)
    cols_copy.start()
    for row in range(AGG):
        k_copy(row).start()

    def one_blank(row, carry):
        for column in range(absent):
            out_ref[row, column] = jnp.zeros((64, 128), jnp.bfloat16)
        return carry

    lax.fori_loop(0, AGG, one_blank, 0)
    cols_copy.wait()

    def one_row(row, carry):
        k_copy(row).wait()
        for slot in range(slots):
            column = cols_ref[half * AGG + row, slot]
            present = (column >= 0) & (column < total_rows)
            place = jnp.where(present, column - first_row + AGG, absent)
            place = jnp.clip(place, 0, absent)
            out_ref[row, place] = jnp.concatenate(split_high_low(k_ref[row, slot]), axis=1)
        return carry

    lax.fori_loop(0, AGG, one_row, 0)


def transpose_blocks(sources, place_ref, p_ref):
    depth = place_ref.shape[1] * place_ref.shape[2] * place_ref.shape[3]
    for side, (source, first) in enumerate(sources):
        for pair in range(PAIRS):
            for window in range(3):
                place_ref[pair, window, side] = source[first + pair, window]
    for pair in range(PAIRS):
        turned = place_ref[pair].reshape(depth, 128).T
        for place, part in enumerate(split_high_low(turned)):
            for sub in range(2):
                p_ref[2 * pair + sub, :, 128 * place : 128 * place + depth] = part[
                    64 * sub : 64 * sub + 64
                ]


def stiff_product(step, k_ref, p_ref):
    rows = []
    blocks = []
    for row in range(AGG):
        rows.append(k_ref[:, step * AGG + row].reshape(AGG * 64, 128))
        blocks += [p_ref[row], p_ref[row]]
    total = jnp.dot(
        jnp.concatenate(rows, axis=1),
        jnp.concatenate(blocks, axis=0),
        preferred_element_type=jnp.float32,
    )
    return split_high_low(total[:, :128] + total[:, 128:])


def stiff_kernel(mine, other, pair_both, k_ref, out_ref, place_ref, p_ref):
    half = lax.axis_index("col") % 2
    for place, step, sources in (
        (0, 1, ((mine, 0), (pair_both, PAIRS))),
        (1, 2 - 2 * half, ((other, 0), (pair_both, 0))),
    ):
        transpose_blocks(sources, place_ref.at[place], p_ref.at[place])
        high, low = stiff_product(step, k_ref, p_ref.at[place])
        out_ref[place, 0] = high
        out_ref[place, 1] = low


def coarse_terms(stiffs, pieces, windows, share, high_ref, low_ref):
    count = len(pieces)
    width = count * share
    depth = 6 * share
    position = lax.axis_index("col")
    first_half = position % 2 == 0
    for place, window in enumerate(windows):
        for shift in range(count):
            first = PAIRS if shift == 1 else 0
            for pair in range(PAIRS):
                high, low = split_high_low(pieces[shift][first + pair, window])
                high_ref[place, pair, position ^ shift] = high
                low_ref[place, pair, position ^ shift] = low

    def rows_of(part):
        return jnp.concatenate(
            [
                jnp.concatenate(
                    [part[place, pair].reshape(width, 128) for pair in range(PAIRS)], axis=1
                )
                for place in range(len(windows))
            ],
            axis=0,
        )

    high, low = rows_of(high_ref), rows_of(low_ref)
    both = jnp.concatenate([high, low], axis=0)
    rows = len(windows) * width
    totals = []
    for stiff_high, stiff_low in stiffs:
        total = jnp.dot(both, stiff_high, preferred_element_type=jnp.float32)
        rest = jnp.dot(high, stiff_low, preferred_element_type=jnp.float32)
        totals.append(total[:rows] + total[rows:] + rest)
    mine, other, near = totals
    steps = (jnp.where(first_half, near, other), mine, jnp.where(first_half, other, near))
    terms = [[None] * 5 for _ in windows]
    for step, total in enumerate(steps):
        for place in range(len(windows)):
            turned = total[width * place : width * place + width].T[:depth]
            turned = turned.reshape(3, 2, share, width)
            for slot in range(3):
                before = terms[place][step + slot]
                terms[place][step + slot] = turned[slot] if before is None else before + turned[slot]
    return terms


def edge_kernel(count, share, k_ref, stiff, *refs):
    pieces = refs[:count]
    near, pair_near, edge_ref, near_ref, place_ref, p_ref, high_ref, low_ref = refs[count:]
    half = lax.axis_index("col") % 2
    transpose_blocks(((near, 0), (pair_near, 0)), place_ref, p_ref)
    high, low = stiff_product(2 * half, k_ref, p_ref)
    near_ref[0] = high
    near_ref[1] = low
    stiffs = [(stiff[place, 0], stiff[place, 1]) for place in range(2)] + [(high, low)]
    (terms,) = coarse_terms(stiffs, pieces, (2 * half,), share, high_ref, low_ref)
    for slot in range(5):
        for side in range(2):
            term = terms[slot][side]
            folded = jnp.concatenate([term[: share // 2], term[share // 2 :]], axis=1)
            edge_ref[5 * side + slot] = folded


def inner_kernel(count, share, stiff, stiff_near, *refs):
    pieces = refs[:count]
    own_ref, pair_ref, high_ref, low_ref = refs[count:]
    half = lax.axis_index("col") % 2
    width = count * share
    stiffs = [(stiff[place, 0], stiff[place, 1]) for place in range(2)]
    stiffs.append((stiff_near[0], stiff_near[1]))
    windows = (1 - half, 2 - half)
    lower, upper = coarse_terms(stiffs, pieces, windows, share, high_ref, low_ref)
    for side, ref in ((0, own_ref), (1, pair_ref)):
        for slot in range(5):
            ref[slot] = jnp.concatenate([lower[slot][side], upper[slot][side]], axis=1)


def sum_kernel(share, own, from_pair, from_edge, from_pair_edge, out_ref):
    half = lax.axis_index("col") % 2
    width = own.shape[2] // 2

    def unfold(folded):
        return jnp.concatenate([folded[:, :width], folded[:, width:]], axis=0)

    def write(lower, upper, before, after):
        for offset in range(7):
            first = [lower[offset - 1][:, :width]] if 1 <= offset < 6 else []
            first += [upper[offset - 2][:, :width]] if 2 <= offset else []
            first += [unfold(before[offset])] if offset < 5 else []
            out_ref[0, offset] = sum(first[1:], first[0])
            second = [lower[offset][:, width:]] if offset < 5 else []
            second += [upper[offset - 1][:, width:]] if 1 <= offset < 6 else []
            second += [unfold(after[offset - 2])] if 2 <= offset else []
            out_ref[1, offset] = sum(second[1:], second[0])

    @pl.when(half == 0)
    def _():
        write(own, from_pair, from_pair_edge, from_edge)

    @pl.when(half == 1)
    def _():
        write(from_pair, own, from_edge, from_pair_edge)


def body(k_vals, k_cols, p_vals, p_cols, *, rows_axis, cols_axis):
    own_rows, slots, fine, _ = k_vals.shape
    share = p_vals.shape[3]
    padded = -(-share // 16) * 16
    total_rows = own_rows * rows_axis
    blocks_all = total_rows // AGG
    width = cols_axis * padded
    vmem = pl.BlockSpec(memory_space=pltpu.VMEM)
    hbm = pl.BlockSpec(memory_space=pltpu.HBM)
    params = pltpu.CompilerParams(vmem_limit_bytes=24 * 1024 * 1024)

    def in_hbm(value):
        return pltpu.with_memory_space_constraint(value, pltpu.HBM)

    def send(value, target):
        perm = []
        for row in range(rows_axis):
            for col in range(cols_axis):
                to_row, to_col = target(row, col)
                perm.append((row * cols_axis + col, to_row * cols_axis + to_col))
        return lax.ppermute(value, ("row", "col"), perm)

    def toward(row, col):
        return (row + (1 if col % 2 == 0 else -1)) % rows_axis, col

    def away(row, col):
        to_row = row - (1 if col % 2 == 0 else -1)
        return (to_row, col) if 0 <= to_row < rows_axis else swap(row, col)

    def swap(row, col):
        return row, col ^ 1

    p_rows = jnp.swapaxes(p_vals, 2, 3)
    if padded != share:
        p_rows = jnp.pad(p_rows, ((0, 0), (0, 0), (0, padded - share), (0, 0)))
    group_shape = jax.ShapeDtypeStruct((PAIRS, 3, padded, 128), jnp.float32)
    both_shape = jax.ShapeDtypeStruct((2 * PAIRS, 3, padded, 128), jnp.float32)
    both, mine, other, mine_again, other_again = pl.pallas_call(
        functools.partial(pack_kernel, blocks_all),
        out_shape=[both_shape] + [group_shape] * 4,
        in_specs=[hbm, hbm],
        out_specs=[vmem] * 5,
        scratch_shapes=[
            pltpu.SMEM(p_cols.T.shape, jnp.int32),
            pltpu.VMEM(p_rows.shape, jnp.float32),
            pltpu.SemaphoreType.DMA((2,)),
        ],
        compiler_params=params,
        name="pack_window",
    )(in_hbm(p_cols.T), in_hbm(p_rows))

    pair_both = send(both, swap)
    pieces = [mine, pair_both]
    for shift in range(2, cols_axis):
        pieces.append(
            send(mine_again if shift % 2 == 0 else other_again, lambda row, col: (row, col ^ shift))
        )
    near = send(other, toward)
    k_split = pl.pallas_call(
        functools.partial(split_kernel, slots, total_rows),
        out_shape=jax.ShapeDtypeStruct((AGG, 3 * AGG + 1, fine, 128), jnp.bfloat16),
        in_specs=[hbm, hbm],
        out_specs=vmem,
        scratch_shapes=[
            pltpu.SMEM(k_cols.shape, jnp.int32),
            pltpu.VMEM((AGG, slots, fine, fine), jnp.float32),
            pltpu.SemaphoreType.DMA,
            pltpu.SemaphoreType.DMA((AGG,)),
        ],
        compiler_params=params,
        cost_estimate=pl.CostEstimate(flops=0, bytes_accessed=8_000_000, transcendentals=0),
        name="split_stiffness",
    )(in_hbm(k_cols), in_hbm(k_vals))

    k_split, pair_both = lax.optimization_barrier((k_split, pair_both))
    pieces[1] = pair_both
    pair_near = send(pair_both[:PAIRS], toward)

    stiff_shape = (2, AGG * fine, 128)
    place_shape = (PAIRS, 3, 2, padded, 128)
    p_shape = (AGG, fine, 256)
    stiff = pl.pallas_call(
        stiff_kernel,
        out_shape=jax.ShapeDtypeStruct((2, *stiff_shape), jnp.bfloat16),
        in_specs=[vmem] * 4,
        out_specs=vmem,
        scratch_shapes=[
            pltpu.VMEM((2, *place_shape), jnp.float32),
            pltpu.VMEM((2, *p_shape), jnp.bfloat16),
        ],
        compiler_params=params,
        cost_estimate=pl.CostEstimate(
            flops=1_000_000_000, bytes_accessed=3_000_000, transcendentals=0
        ),
        name="stiff_prolong",
    )(mine, other, pair_both, k_split)

    def part_scratch(windows):
        return [pltpu.VMEM((windows, PAIRS, cols_axis, padded, 128), jnp.bfloat16)] * 2

    edge, stiff_near = pl.pallas_call(
        functools.partial(edge_kernel, cols_axis, padded),
        out_shape=[
            jax.ShapeDtypeStruct((10, padded // 2, 2 * width), jnp.float32),
            jax.ShapeDtypeStruct(stiff_shape, jnp.bfloat16),
        ],
        in_specs=[vmem] * (4 + cols_axis),
        out_specs=[vmem] * 2,
        scratch_shapes=[pltpu.VMEM(place_shape, jnp.float32), pltpu.VMEM(p_shape, jnp.bfloat16)]
        + part_scratch(1),
        compiler_params=params,
        cost_estimate=pl.CostEstimate(
            flops=1_000_000_000, bytes_accessed=2_000_000, transcendentals=0
        ),
        name="edge_terms",
    )(k_split, stiff, *pieces, near, pair_near)
    from_edge = send(edge, away)

    band_shape = jax.ShapeDtypeStruct((5, padded, 2 * width), jnp.float32)
    own, for_pair = pl.pallas_call(
        functools.partial(inner_kernel, cols_axis, padded),
        out_shape=[band_shape] * 2,
        in_specs=[vmem] * (2 + cols_axis),
        out_specs=[vmem] * 2,
        scratch_shapes=part_scratch(2),
        compiler_params=params,
        cost_estimate=pl.CostEstimate(
            flops=500_000_000, bytes_accessed=1_000_000, transcendentals=0
        ),
        name="inner_terms",
    )(stiff, stiff_near, *pieces)
    from_pair = send(for_pair, swap)
    from_pair_edge = send(from_edge[5:], swap)

    coarse = pl.pallas_call(
        functools.partial(sum_kernel, padded),
        out_shape=jax.ShapeDtypeStruct((2, 7, padded, width), jnp.float32),
        in_specs=[vmem] * 4,
        out_specs=vmem,
        compiler_params=params,
        name="sum_terms",
    )(own, from_pair, from_edge, from_pair_edge)
    if padded != share:
        coarse = coarse.reshape(2, 7, padded, cols_axis, padded)[:, :, :share, :, :share]
        coarse = coarse.reshape(2, 7, share, cols_axis * share)
    return jnp.swapaxes(coarse, 2, 3)


def solution(mesh):
    placed = (
        P("row", None, None, None),
        P("row", None),
        P("row", None, None, "col"),
        P("row", None),
    )
    return jax.shard_map(
        functools.partial(body, rows_axis=mesh.shape["row"], cols_axis=mesh.shape["col"]),
        mesh=mesh,
        in_specs=placed,
        out_specs=P("row", None, None, "col"),
        check_vma=False,
    )
```

time: 114 us -> 24.5 us (0.21)
  the two profiles are of different devices: /device:TPU:27 before, /device:TPU:0 now
where the time goes in v1:
time: 24.5 us; the launch traced here: 24.3 us
  waiting for transfers between devices  8.92 us (36%)
  starting transfers between devices  8.49 us (35%)
  Pallas kernels  6.87 us (28%)
    ppermute x8, waiting for transfers between devices, send(): return lax.ppermute(value, ('row', 'col'), perm)  8.92 us
    ppermute x8, starting transfers between devices, send(): return lax.ppermute(value, ('row', 'col'), perm)  8.49 us
    pallas_call x1, Pallas kernels, body(): pl.pallas_call(functools.partial(split_kernel, slots, total_rows), out_sh...  2.28 us
    pallas_call x1, Pallas kernels, body(): pl.pallas_call(functools.partial(pack_kernel, blocks_all), out_shape=[bot...  1.18 us
    pallas_call x1, Pallas kernels, body(): pl.pallas_call(functools.partial(edge_kernel, cols_axis, padded), out_sha...  1.09 us
    pallas_call x1, Pallas kernels, body(): pl.pallas_call(functools.partial(sum_kernel, padded), out_shape=jax.Shape...  0.86 us
    pallas_call x1, Pallas kernels, body(): pl.pallas_call(stiff_kernel, out_shape=jax.ShapeDtypeStruct((2, *stiff_sh...  0.84 us
    pallas_call x1, Pallas kernels, body(): pl.pallas_call(functools.partial(inner_kernel, cols_axis, padded), out_sh...  0.63 us
  transfers between devices with their start and end apart: 8, of which 6 were waited for; matrix products, arithmetic and copies ran while one was open for 0% of the time, Pallas kernels for 15%

profile of v1, /device:TPU:0, one launch (start us, length us, event | category | flops | bytes accessed | tf_op | source)
XLA Modules:
  0.0 24.3 jit_solution(936435864309343218)
XLA Ops:
  0.0 1.2 %pack_window.1 = (f32[8,3,16,128]{3,2,1,0:T(8,128)S(1)}, f32[4,3,16,128]{3,2,1,0:T(8,128)S(1)}, f32[4,3,16,128]{3,2,1,0:T(8,128)S(1)}, f32[4,3,16,128]{3,2,1,0:T(8,128)S(1)}, f32[4,3,16,128]{3,2,1,0:T(8,128)S(1)}) custom-call(s32[3,16]{1,0:T(4,128)} %bitcast.4, f32[16,3,16,64]{3,2,1,0:T(8,128)} %bitcast.3), custom_call_target="tpu_custom_call" | custom-call | tf_op jit(solution)/shard_map/pack_window/pallas_call | solution.py:273
  1.2 3.1 %collective-permute-start = (f32[8,3,16,128]{3,2,1,0:T(8,128)S(1)}, f32[8,3,16,128]{3,2,1,0:T(8,128)S(1)}, u32[]{:S(2)}, u32[]{:S(2)}) collective-permute-start(f32[8,3,16,128]{3,2,1,0:T(8,128)S(1)} %get-tuple-element.18), channel_id=1, source_target_pairs={{0,1},{1,0},{2,3},{3,2},{4,5},{5,4},{6,7},{7,6},{8,9},{9,8},{10,11... | collective-permute-start | bytes 589832 | tf_op jit(solution)/shard_map/ppermute | solution.py:256
  4.3 2.6 %collective-permute-start.1 = (f32[4,3,16,128]{3,2,1,0:T(8,128)S(1)}, f32[4,3,16,128]{3,2,1,0:T(8,128)S(1)}, u32[]{:S(2)}, u32[]{:S(2)}) collective-permute-start(f32[4,3,16,128]{3,2,1,0:T(8,128)S(1)} %get-tuple-element.21), channel_id=1, source_target_pairs={{0,2},{1,3},{2,0},{3,1},{4,6},{5,7},{6,4},{7,5},{8,10},{9,11},{10,... | collective-permute-start | bytes 294920 | tf_op jit(solution)/shard_map/ppermute | solution.py:256
  6.9 0.0 collective-permute-start.2
  6.9 0.0 collective-permute-start.3
  6.9 2.3 %split_stiffness.1.k_ref = bf16[8,25,64,128]{3,2,1,0:T(8,128)(2,1)S(1)} custom-call(s32[16,15]{1,0:T(8,128)} %cols_hbm.1, f32[16,15,64,64]{3,2,1,0:T(8,128)} %k_hbm.1), custom_call_target="tpu_custom_call" | custom-call | bytes 8000000 | tf_op jit(solution)/shard_map/split_stiffness/pallas_call | solution.py:294
  9.2 2.1 %collective-permute-done.pair_both.refs_1_ = f32[8,3,16,128]{3,2,1,0:T(8,128)S(1)} collective-permute-done((f32[8,3,16,128]{3,2,1,0:T(8,128)S(1)}, f32[8,3,16,128]{3,2,1,0:T(8,128)S(1)}, u32[]{:S(2)}, u32[]{:S(2)}) %collective-permute-start) | collective-permute-done | bytes 196640 | tf_op jit(solution)/shard_map/ppermute | solution.py:256
  11.3 0.1 collective-permute-start.4
  11.4 0.8 %stiff_prolong.1.stiff = bf16[2,2,512,128]{3,2,1,0:T(8,128)(2,1)S(1)} custom-call(f32[4,3,16,128]{3,2,1,0:T(8,128)S(1)} %get-tuple-element.16.mine.refs_0_, f32[4,3,16,128]{3,2,1,0:T(8,128)S(1)} %get-tuple-element.17.other, f32[8,3,16,128]{3,2,1,0:T(8,128)S(1)} %collective-permute-done.pair_both.refs_1_, bf16[8,25,64,128]{3,2,1,0:T(8,128)(2,1)S(1)} %split_stiffness.1.k_ref), custom_call_target="tpu_custom_call" | custom-call | flops 1000000000 | bytes 3000000 | tf_op jit(solution)/shard_map/stiff_prolong/pallas_call | solution.py:317
  12.2 0.0 collective-permute-done.1.refs_2_
  12.2 3.5 %collective-permute-done.2.refs_3_ = f32[4,3,16,128]{3,2,1,0:T(8,128)S(1)} collective-permute-done((f32[4,3,16,128]{3,2,1,0:T(8,128)S(1)}, f32[4,3,16,128]{3,2,1,0:T(8,128)S(1)}, u32[]{:S(2)}, u32[]{:S(2)}) %collective-permute-start.2) | collective-permute-done | bytes 98336 | tf_op jit(solution)/shard_map/ppermute | solution.py:256
  15.7 0.0 collective-permute-done.3.refs_4_
  15.7 0.6 %collective-permute-done.4.refs_5_ = f32[4,3,16,128]{3,2,1,0:T(8,128)S(1)} collective-permute-done((f32[4,3,16,128]{3,2,1,0:T(8,128)S(1)}, f32[4,3,16,128]{3,2,1,0:T(8,128)S(1)}, u32[]{:S(2)}, u32[]{:S(2)}) %collective-permute-start.4) | collective-permute-done | bytes 98336 | tf_op jit(solution)/shard_map/ppermute | solution.py:256
  16.3 1.1 %edge_terms.1 = (f32[10,8,128]{2,1,0:T(8,128)S(1)}, bf16[2,512,128]{2,1,0:T(8,128)(2,1)S(1)}) custom-call(bf16[8,25,64,128]{3,2,1,0:T(8,128)(2,1)S(1)} %split_stiffness.1.k_ref, bf16[2,2,512,128]{3,2,1,0:T(8,128)(2,1)S(1)} %stiff_prolong.1.stiff, f32[4,3,16,128]{3,2,1,0:T(8,128)S(1)} %get-tuple-element.16.mine.refs_0_, ...), custom_call_target="tpu_custom_call" | custom-call | flops 1000000000 | bytes 2000000 | tf_op jit(solution)/shard_map/edge_terms/pallas_call | solution.py:336
  17.4 0.3 %collective-permute-start.6 = (f32[10,8,128]{2,1,0:T(8,128)S(1)}, f32[10,8,128]{2,1,0:T(8,128)S(1)}, u32[]{:S(2)}, u32[]{:S(2)}) collective-permute-start(f32[10,8,128]{2,1,0:T(8,128)S(1)} %get-tuple-element.26), channel_id=1, source_target_pairs={{0,1},{1,5},{2,3},{3,7},{4,0},{5,9},{6,2},{7,11},{8,4},{9,13},{10,... | collective-permute-start | bytes 122888 | tf_op jit(solution)/shard_map/ppermute | solution.py:256
  17.7 0.6 %inner_terms.1 = (f32[5,16,128]{2,1,0:T(8,128)S(1)}, f32[5,16,128]{2,1,0:T(8,128)S(1)}) custom-call(bf16[2,2,512,128]{3,2,1,0:T(8,128)(2,1)S(1)} %stiff_prolong.1.stiff, bf16[2,512,128]{2,1,0:T(8,128)(2,1)S(1)} %get-tuple-element.23.stiff_near, f32[4,3,16,128]{3,2,1,0:T(8,128)S(1)} %get-tuple-element.16.mine.refs_0_, ...), custom_call_target="tpu_custom_call" | custom-call | flops 500000000 | bytes 1000000 | tf_op jit(solution)/shard_map/inner_terms/pallas_call | solution.py:355
  18.4 0.1 collective-permute-start.5
  18.4 1.0 %collective-permute-done.6.from_edge = f32[10,8,128]{2,1,0:T(8,128)S(1)} collective-permute-done((f32[10,8,128]{2,1,0:T(8,128)S(1)}, f32[10,8,128]{2,1,0:T(8,128)S(1)}, u32[]{:S(2)}, u32[]{:S(2)}) %collective-permute-start.6) | collective-permute-done | bytes 40992 | tf_op jit(solution)/shard_map/ppermute | solution.py:256
  19.4 2.3 %collective-permute-start.7 = (f32[5,8,128]{2,1,0:T(8,128)S(1)}, f32[5,8,128]{2,1,0:T(8,128)S(1)}, u32[]{:S(2)}, u32[]{:S(2)}) collective-permute-start(f32[5,8,128]{2,1,0:T(8,128)S(1)} %slice.8), channel_id=1, source_target_pairs={{0,1},{1,0},{2,3},{3,2},{4,5},{5,4},{6,7},{7,6},{8,9},{9,8},{10,11... | collective-permute-start | bytes 61448 | tf_op jit(solution)/shard_map/ppermute | solution.py:256
  21.7 0.7 %collective-permute-done.5.from_pair = f32[5,16,128]{2,1,0:T(8,128)S(1)} collective-permute-done((f32[5,16,128]{2,1,0:T(8,128)S(1)}, f32[5,16,128]{2,1,0:T(8,128)S(1)}, u32[]{:S(2)}, u32[]{:S(2)}) %collective-permute-start.5) | collective-permute-done | bytes 40992 | tf_op jit(solution)/shard_map/ppermute | solution.py:256
  22.4 1.1 %collective-permute-done.7.from_pair_edge = f32[5,8,128]{2,1,0:T(8,128)S(1)} collective-permute-done((f32[5,8,128]{2,1,0:T(8,128)S(1)}, f32[5,8,128]{2,1,0:T(8,128)S(1)}, u32[]{:S(2)}, u32[]{:S(2)}) %collective-permute-start.7) | collective-permute-done | bytes 20512 | tf_op jit(solution)/shard_map/ppermute | solution.py:256
  23.5 0.9 %sum_terms.1 = f32[2,7,16,64]{3,2,1,0:T(8,128)} custom-call(f32[5,16,128]{2,1,0:T(8,128)S(1)} %get-tuple-element.24.own, f32[5,16,128]{2,1,0:T(8,128)S(1)} %collective-permute-done.5.from_pair, f32[10,8,128]{2,1,0:T(8,128)S(1)} %collective-permute-done.6.from_edge, f32[5,8,128]{2,1,0:T(8,128)S(1)} %collective-permute-done.7.from_pair_edge), custom_call_target="tpu_custom_call" | custom-call | tf_op jit(solution)/shard_map/sum_terms/pallas_call | solution.py:370
  (2 shorter events, 0.0 us)
Async XLA Ops:
  1.2 10.1 %collective-permute-start = (f32[8,3,16,128]{3,2,1,0:T(8,128)S(1)}, f32[8,3,16,128]{3,2,1,0:T(8,128)S(1)}, u32[]{:S(2)}, u32[]{:S(2)}) collective-permute-start(f32[8,3,16,128]{3,2,1,0:T(8,128)S(1)} %get-tuple-element.18), channel_id=1, source_target_pairs={{0,1},{1,0},{2,3},{3,2},{4,5},{5,4},{6,7},{7,6},{8,9},{9,8},{10,11... | collective-permute-start | bytes 589832 | tf_op jit(solution)/shard_map/ppermute | solution.py:256
  4.3 7.9 %collective-permute-start.1 = (f32[4,3,16,128]{3,2,1,0:T(8,128)S(1)}, f32[4,3,16,128]{3,2,1,0:T(8,128)S(1)}, u32[]{:S(2)}, u32[]{:S(2)}) collective-permute-start(f32[4,3,16,128]{3,2,1,0:T(8,128)S(1)} %get-tuple-element.21), channel_id=1, source_target_pairs={{0,2},{1,3},{2,0},{3,1},{4,6},{5,7},{6,4},{7,5},{8,10},{9,11},{10,... | collective-permute-start | bytes 294920 | tf_op jit(solution)/shard_map/ppermute | solution.py:256
  6.9 8.8 %collective-permute-start.2 = (f32[4,3,16,128]{3,2,1,0:T(8,128)S(1)}, f32[4,3,16,128]{3,2,1,0:T(8,128)S(1)}, u32[]{:S(2)}, u32[]{:S(2)}) collective-permute-start(f32[4,3,16,128]{3,2,1,0:T(8,128)S(1)} %get-tuple-element.22), channel_id=1, source_target_pairs={{0,3},{1,2},{2,1},{3,0},{4,7},{5,6},{6,5},{7,4},{8,11},{9,10},{10,... | collective-permute-start | bytes 294920 | tf_op jit(solution)/shard_map/ppermute | solution.py:256
  6.9 8.8 %collective-permute-start.3 = (f32[4,3,16,128]{3,2,1,0:T(8,128)S(1)}, f32[4,3,16,128]{3,2,1,0:T(8,128)S(1)}, u32[]{:S(2)}, u32[]{:S(2)}) collective-permute-start(f32[4,3,16,128]{3,2,1,0:T(8,128)S(1)} %get-tuple-element.17.other), channel_id=1, source_target_pairs={{0,4},{1,29},{2,6},{3,31},{4,8},{5,1},{6,10},{7,3},{8,12},{9,5},{1... | collective-permute-start | bytes 294920 | tf_op jit(solution)/shard_map/ppermute | solution.py:256
  11.3 5.0 %collective-permute-start.4 = (f32[4,3,16,128]{3,2,1,0:T(8,128)S(1)}, f32[4,3,16,128]{3,2,1,0:T(8,128)S(1)}, u32[]{:S(2)}, u32[]{:S(2)}) collective-permute-start(f32[4,3,16,128]{3,2,1,0:T(8,128)S(1)} %slice.6), channel_id=1, source_target_pairs={{0,4},{1,29},{2,6},{3,31},{4,8},{5,1},{6,10},{7,3},{8,12},{9,5},{1... | collective-permute-start | bytes 294920 | tf_op jit(solution)/shard_map/ppermute | solution.py:256
  17.4 2.0 %collective-permute-start.6 = (f32[10,8,128]{2,1,0:T(8,128)S(1)}, f32[10,8,128]{2,1,0:T(8,128)S(1)}, u32[]{:S(2)}, u32[]{:S(2)}) collective-permute-start(f32[10,8,128]{2,1,0:T(8,128)S(1)} %get-tuple-element.26), channel_id=1, source_target_pairs={{0,1},{1,5},{2,3},{3,7},{4,0},{5,9},{6,2},{7,11},{8,4},{9,13},{10,... | collective-permute-start | bytes 122888 | tf_op jit(solution)/shard_map/ppermute | solution.py:256
  18.4 4.1 %collective-permute-start.5 = (f32[5,16,128]{2,1,0:T(8,128)S(1)}, f32[5,16,128]{2,1,0:T(8,128)S(1)}, u32[]{:S(2)}, u32[]{:S(2)}) collective-permute-start(f32[5,16,128]{2,1,0:T(8,128)S(1)} %get-tuple-element.25), channel_id=1, source_target_pairs={{0,1},{1,0},{2,3},{3,2},{4,5},{5,4},{6,7},{7,6},{8,9},{9,8},{10,11... | collective-permute-start | bytes 122888 | tf_op jit(solution)/shard_map/ppermute | solution.py:256
  19.4 4.1 %collective-permute-start.7 = (f32[5,8,128]{2,1,0:T(8,128)S(1)}, f32[5,8,128]{2,1,0:T(8,128)S(1)}, u32[]{:S(2)}, u32[]{:S(2)}) collective-permute-start(f32[5,8,128]{2,1,0:T(8,128)S(1)} %slice.8), channel_id=1, source_target_pairs={{0,1},{1,0},{2,3},{3,2},{4,5},{5,4},{6,7},{7,6},{8,9},{9,8},{10,11... | collective-permute-start | bytes 61448 | tf_op jit(solution)/shard_map/ppermute | solution.py:256

commit v2 on v1

--- a/solution.py
+++ b/solution.py
@@ -176,7 +176,7 @@
 
 
 def edge_kernel(count, share, k_ref, stiff, *refs):
-    pieces = refs[:count]
+    pieces = [*refs[:2], *refs[2:count][::-1]]
     near, pair_near, edge_ref, near_ref, place_ref, p_ref, high_ref, low_ref = refs[count:]
     half = lax.axis_index("col") % 2
     transpose_blocks(((near, 0), (pair_near, 0)), place_ref, p_ref)
@@ -193,7 +193,7 @@
 
 
 def inner_kernel(count, share, stiff, stiff_near, *refs):
-    pieces = refs[:count]
+    pieces = [*refs[:2], *refs[2:count][::-1]]
     own_ref, pair_ref, high_ref, low_ref = refs[count:]
     half = lax.axis_index("col") % 2
     width = count * share
@@ -310,6 +310,7 @@
     k_split, pair_both = lax.optimization_barrier((k_split, pair_both))
     pieces[1] = pair_both
     pair_near = send(pair_both[:PAIRS], toward)
+    pieces = [*pieces[:2], *pieces[2:][::-1]]
 
     stiff_shape = (2, AGG * fine, 128)
     place_shape = (PAIRS, 3, 2, padded, 128)

time: 24.5 us -> 24.3 us (level)
  waiting for transfers between devices: 8.92 us -> 7.54 us
  starting transfers between devices: 8.49 us -> 9.7 us
    ppermute x8, waiting for transfers between devices: 8.92 us -> 7.54 us  [send(): return lax.ppermute(value, ('row', 'col'), perm)]
    ppermute x8, starting transfers between devices: 8.49 us -> 9.7 us  [send(): return lax.ppermute(value, ('row', 'col'), perm)]
where the time goes in v2:
time: 24.3 us; the launch traced here: 24.2 us
  starting transfers between devices  9.7 us (40%)
  waiting for transfers between devices  7.54 us (31%)
  Pallas kernels  6.87 us (28%)
    ppermute x8, starting transfers between devices, send(): return lax.ppermute(value, ('row', 'col'), perm)  9.7 us
    ppermute x8, waiting for transfers between devices, send(): return lax.ppermute(value, ('row', 'col'), perm)  7.54 us
    pallas_call x1, Pallas kernels, body(): pl.pallas_call(functools.partial(split_kernel, slots, total_rows), out_sh...  2.28 us
    pallas_call x1, Pallas kernels, body(): pl.pallas_call(functools.partial(pack_kernel, blocks_all), out_shape=[bot...  1.18 us
    pallas_call x1, Pallas kernels, body(): pl.pallas_call(functools.partial(edge_kernel, cols_axis, padded), out_sha...  1.09 us
    pallas_call x1, Pallas kernels, body(): pl.pallas_call(functools.partial(sum_kernel, padded), out_shape=jax.Shape...  0.86 us
    pallas_call x1, Pallas kernels, body(): pl.pallas_call(stiff_kernel, out_shape=jax.ShapeDtypeStruct((2, *stiff_sh...  0.83 us
    pallas_call x1, Pallas kernels, body(): pl.pallas_call(functools.partial(inner_kernel, cols_axis, padded), out_sh...  0.63 us
  transfers between devices with their start and end apart: 8, of which 6 were waited for; matrix products, arithmetic and copies ran while one was open for 0% of the time, Pallas kernels for 15%

profile of v2, /device:TPU:0, one launch (start us, length us, event | category | flops | bytes accessed | tf_op | source)
XLA Modules:
  0.0 24.2 jit_solution(6266308570905415633)
XLA Ops:
  0.0 1.2 %pack_window.1 = (f32[8,3,16,128]{3,2,1,0:T(8,128)S(1)}, f32[4,3,16,128]{3,2,1,0:T(8,128)S(1)}, f32[4,3,16,128]{3,2,1,0:T(8,128)S(1)}, f32[4,3,16,128]{3,2,1,0:T(8,128)S(1)}, f32[4,3,16,128]{3,2,1,0:T(8,128)S(1)}) custom-call(s32[3,16]{1,0:T(4,128)} %bitcast.4, f32[16,3,16,64]{3,2,1,0:T(8,128)} %bitcast.3), custom_call_target="tpu_custom_call" | custom-call | tf_op jit(solution)/shard_map/pack_window/pallas_call | solution.py:273
  1.2 3.1 %collective-permute-start = (f32[8,3,16,128]{3,2,1,0:T(8,128)S(1)}, f32[8,3,16,128]{3,2,1,0:T(8,128)S(1)}, u32[]{:S(2)}, u32[]{:S(2)}) collective-permute-start(f32[8,3,16,128]{3,2,1,0:T(8,128)S(1)} %get-tuple-element.18), channel_id=1, source_target_pairs={{0,1},{1,0},{2,3},{3,2},{4,5},{5,4},{6,7},{7,6},{8,9},{9,8},{10,11... | collective-permute-start | bytes 589832 | tf_op jit(solution)/shard_map/ppermute | solution.py:256
  4.3 2.5 %collective-permute-start.1 = (f32[4,3,16,128]{3,2,1,0:T(8,128)S(1)}, f32[4,3,16,128]{3,2,1,0:T(8,128)S(1)}, u32[]{:S(2)}, u32[]{:S(2)}) collective-permute-start(f32[4,3,16,128]{3,2,1,0:T(8,128)S(1)} %get-tuple-element.21), channel_id=1, source_target_pairs={{0,3},{1,2},{2,1},{3,0},{4,7},{5,6},{6,5},{7,4},{8,11},{9,10},{10,... | collective-permute-start | bytes 294920 | tf_op jit(solution)/shard_map/ppermute | solution.py:256
  6.8 0.1 collective-permute-start.2
  6.9 0.0 collective-permute-start.3
  6.9 2.3 %split_stiffness.1.k_ref = bf16[8,25,64,128]{3,2,1,0:T(8,128)(2,1)S(1)} custom-call(s32[16,15]{1,0:T(8,128)} %cols_hbm.1, f32[16,15,64,64]{3,2,1,0:T(8,128)} %k_hbm.1), custom_call_target="tpu_custom_call" | custom-call | bytes 8000000 | tf_op jit(solution)/shard_map/split_stiffness/pallas_call | solution.py:294
  9.2 0.4 %collective-permute-done.pair_both.refs_1_ = f32[8,3,16,128]{3,2,1,0:T(8,128)S(1)} collective-permute-done((f32[8,3,16,128]{3,2,1,0:T(8,128)S(1)}, f32[8,3,16,128]{3,2,1,0:T(8,128)S(1)}, u32[]{:S(2)}, u32[]{:S(2)}) %collective-permute-start) | collective-permute-done | bytes 196640 | tf_op jit(solution)/shard_map/ppermute | solution.py:256
  9.6 1.2 %collective-permute-start.4 = (f32[4,3,16,128]{3,2,1,0:T(8,128)S(1)}, f32[4,3,16,128]{3,2,1,0:T(8,128)S(1)}, u32[]{:S(2)}, u32[]{:S(2)}) collective-permute-start(f32[4,3,16,128]{3,2,1,0:T(8,128)S(1)} %slice.6), channel_id=1, source_target_pairs={{0,4},{1,29},{2,6},{3,31},{4,8},{5,1},{6,10},{7,3},{8,12},{9,5},{1... | collective-permute-start | bytes 294920 | tf_op jit(solution)/shard_map/ppermute | solution.py:256
  10.8 0.8 %stiff_prolong.1.stiff = bf16[2,2,512,128]{3,2,1,0:T(8,128)(2,1)S(1)} custom-call(f32[4,3,16,128]{3,2,1,0:T(8,128)S(1)} %get-tuple-element.16.mine.refs_0_, f32[4,3,16,128]{3,2,1,0:T(8,128)S(1)} %get-tuple-element.17.other, f32[8,3,16,128]{3,2,1,0:T(8,128)S(1)} %collective-permute-done.pair_both.refs_1_, bf16[8,25,64,128]{3,2,1,0:T(8,128)(2,1)S(1)} %split_stiffness.1.k_ref), custom_call_target="tpu_custom_call" | custom-call | flops 1000000000 | bytes 3000000 | tf_op jit(solution)/shard_map/stiff_prolong/pallas_call | solution.py:318
  11.7 2.9 %collective-permute-done.1.refs_2_ = f32[4,3,16,128]{3,2,1,0:T(8,128)S(1)} collective-permute-done((f32[4,3,16,128]{3,2,1,0:T(8,128)S(1)}, f32[4,3,16,128]{3,2,1,0:T(8,128)S(1)}, u32[]{:S(2)}, u32[]{:S(2)}) %collective-permute-start.1) | collective-permute-done | bytes 98336 | tf_op jit(solution)/shard_map/ppermute | solution.py:256
  14.6 1.4 %collective-permute-done.2.refs_3_ = f32[4,3,16,128]{3,2,1,0:T(8,128)S(1)} collective-permute-done((f32[4,3,16,128]{3,2,1,0:T(8,128)S(1)}, f32[4,3,16,128]{3,2,1,0:T(8,128)S(1)}, u32[]{:S(2)}, u32[]{:S(2)}) %collective-permute-start.2) | collective-permute-done | bytes 98336 | tf_op jit(solution)/shard_map/ppermute | solution.py:256
  16.0 0.0 collective-permute-done.3.refs_4_
  16.0 0.0 collective-permute-done.4.refs_5_
  16.0 1.1 %edge_terms.1 = (f32[10,8,128]{2,1,0:T(8,128)S(1)}, bf16[2,512,128]{2,1,0:T(8,128)(2,1)S(1)}) custom-call(bf16[8,25,64,128]{3,2,1,0:T(8,128)(2,1)S(1)} %split_stiffness.1.k_ref, bf16[2,2,512,128]{3,2,1,0:T(8,128)(2,1)S(1)} %stiff_prolong.1.stiff, f32[4,3,16,128]{3,2,1,0:T(8,128)S(1)} %get-tuple-element.16.mine.refs_0_, ...), custom_call_target="tpu_custom_call" | custom-call | flops 1000000000 | bytes 2000000 | tf_op jit(solution)/shard_map/edge_terms/pallas_call | solution.py:337
  17.1 0.3 %collective-permute-start.6 = (f32[10,8,128]{2,1,0:T(8,128)S(1)}, f32[10,8,128]{2,1,0:T(8,128)S(1)}, u32[]{:S(2)}, u32[]{:S(2)}) collective-permute-start(f32[10,8,128]{2,1,0:T(8,128)S(1)} %get-tuple-element.26), channel_id=1, source_target_pairs={{0,1},{1,5},{2,3},{3,7},{4,0},{5,9},{6,2},{7,11},{8,4},{9,13},{10,... | collective-permute-start | bytes 122888 | tf_op jit(solution)/shard_map/ppermute | solution.py:256
  17.4 0.6 %inner_terms.1 = (f32[5,16,128]{2,1,0:T(8,128)S(1)}, f32[5,16,128]{2,1,0:T(8,128)S(1)}) custom-call(bf16[2,2,512,128]{3,2,1,0:T(8,128)(2,1)S(1)} %stiff_prolong.1.stiff, bf16[2,512,128]{2,1,0:T(8,128)(2,1)S(1)} %get-tuple-element.23.stiff_near, f32[4,3,16,128]{3,2,1,0:T(8,128)S(1)} %get-tuple-element.16.mine.refs_0_, ...), custom_call_target="tpu_custom_call" | custom-call | flops 500000000 | bytes 1000000 | tf_op jit(solution)/shard_map/inner_terms/pallas_call | solution.py:356
  18.0 0.1 collective-permute-start.5
  18.2 0.9 %collective-permute-done.6.from_edge = f32[10,8,128]{2,1,0:T(8,128)S(1)} collective-permute-done((f32[10,8,128]{2,1,0:T(8,128)S(1)}, f32[10,8,128]{2,1,0:T(8,128)S(1)}, u32[]{:S(2)}, u32[]{:S(2)}) %collective-permute-start.6) | collective-permute-done | bytes 40992 | tf_op jit(solution)/shard_map/ppermute | solution.py:256
  19.1 2.3 %collective-permute-start.7 = (f32[5,8,128]{2,1,0:T(8,128)S(1)}, f32[5,8,128]{2,1,0:T(8,128)S(1)}, u32[]{:S(2)}, u32[]{:S(2)}) collective-permute-start(f32[5,8,128]{2,1,0:T(8,128)S(1)} %slice.8), channel_id=1, source_target_pairs={{0,1},{1,0},{2,3},{3,2},{4,5},{5,4},{6,7},{7,6},{8,9},{9,8},{10,11... | collective-permute-start | bytes 61448 | tf_op jit(solution)/shard_map/ppermute | solution.py:256
  21.4 0.7 %collective-permute-done.5.from_pair = f32[5,16,128]{2,1,0:T(8,128)S(1)} collective-permute-done((f32[5,16,128]{2,1,0:T(8,128)S(1)}, f32[5,16,128]{2,1,0:T(8,128)S(1)}, u32[]{:S(2)}, u32[]{:S(2)}) %collective-permute-start.5) | collective-permute-done | bytes 40992 | tf_op jit(solution)/shard_map/ppermute | solution.py:256
  22.1 1.2 %collective-permute-done.7.from_pair_edge = f32[5,8,128]{2,1,0:T(8,128)S(1)} collective-permute-done((f32[5,8,128]{2,1,0:T(8,128)S(1)}, f32[5,8,128]{2,1,0:T(8,128)S(1)}, u32[]{:S(2)}, u32[]{:S(2)}) %collective-permute-start.7) | collective-permute-done | bytes 20512 | tf_op jit(solution)/shard_map/ppermute | solution.py:256
  23.3 0.9 %sum_terms.1 = f32[2,7,16,64]{3,2,1,0:T(8,128)} custom-call(f32[5,16,128]{2,1,0:T(8,128)S(1)} %get-tuple-element.24.own, f32[5,16,128]{2,1,0:T(8,128)S(1)} %collective-permute-done.5.from_pair, f32[10,8,128]{2,1,0:T(8,128)S(1)} %collective-permute-done.6.from_edge, f32[5,8,128]{2,1,0:T(8,128)S(1)} %collective-permute-done.7.from_pair_edge), custom_call_target="tpu_custom_call" | custom-call | tf_op jit(solution)/shard_map/sum_terms/pallas_call | solution.py:371
  (2 shorter events, 0.0 us)
Async XLA Ops:
  1.2 8.4 %collective-permute-start = (f32[8,3,16,128]{3,2,1,0:T(8,128)S(1)}, f32[8,3,16,128]{3,2,1,0:T(8,128)S(1)}, u32[]{:S(2)}, u32[]{:S(2)}) collective-permute-start(f32[8,3,16,128]{3,2,1,0:T(8,128)S(1)} %get-tuple-element.18), channel_id=1, source_target_pairs={{0,1},{1,0},{2,3},{3,2},{4,5},{5,4},{6,7},{7,6},{8,9},{9,8},{10,11... | collective-permute-start | bytes 589832 | tf_op jit(solution)/shard_map/ppermute | solution.py:256
  4.3 10.3 %collective-permute-start.1 = (f32[4,3,16,128]{3,2,1,0:T(8,128)S(1)}, f32[4,3,16,128]{3,2,1,0:T(8,128)S(1)}, u32[]{:S(2)}, u32[]{:S(2)}) collective-permute-start(f32[4,3,16,128]{3,2,1,0:T(8,128)S(1)} %get-tuple-element.21), channel_id=1, source_target_pairs={{0,3},{1,2},{2,1},{3,0},{4,7},{5,6},{6,5},{7,4},{8,11},{9,10},{10,... | collective-permute-start | bytes 294920 | tf_op jit(solution)/shard_map/ppermute | solution.py:256
  6.8 9.2 %collective-permute-start.2 = (f32[4,3,16,128]{3,2,1,0:T(8,128)S(1)}, f32[4,3,16,128]{3,2,1,0:T(8,128)S(1)}, u32[]{:S(2)}, u32[]{:S(2)}) collective-permute-start(f32[4,3,16,128]{3,2,1,0:T(8,128)S(1)} %get-tuple-element.22), channel_id=1, source_target_pairs={{0,2},{1,3},{2,0},{3,1},{4,6},{5,7},{6,4},{7,5},{8,10},{9,11},{10,... | collective-permute-start | bytes 294920 | tf_op jit(solution)/shard_map/ppermute | solution.py:256
  6.9 9.1 %collective-permute-start.3 = (f32[4,3,16,128]{3,2,1,0:T(8,128)S(1)}, f32[4,3,16,128]{3,2,1,0:T(8,128)S(1)}, u32[]{:S(2)}, u32[]{:S(2)}) collective-permute-start(f32[4,3,16,128]{3,2,1,0:T(8,128)S(1)} %get-tuple-element.17.other), channel_id=1, source_target_pairs={{0,4},{1,29},{2,6},{3,31},{4,8},{5,1},{6,10},{7,3},{8,12},{9,5},{1... | collective-permute-start | bytes 294920 | tf_op jit(solution)/shard_map/ppermute | solution.py:256
  9.6 6.4 %collective-permute-start.4 = (f32[4,3,16,128]{3,2,1,0:T(8,128)S(1)}, f32[4,3,16,128]{3,2,1,0:T(8,128)S(1)}, u32[]{:S(2)}, u32[]{:S(2)}) collective-permute-start(f32[4,3,16,128]{3,2,1,0:T(8,128)S(1)} %slice.6), channel_id=1, source_target_pairs={{0,4},{1,29},{2,6},{3,31},{4,8},{5,1},{6,10},{7,3},{8,12},{9,5},{1... | collective-permute-start | bytes 294920 | tf_op jit(solution)/shard_map/ppermute | solution.py:256
  17.1 2.0 %collective-permute-start.6 = (f32[10,8,128]{2,1,0:T(8,128)S(1)}, f32[10,8,128]{2,1,0:T(8,128)S(1)}, u32[]{:S(2)}, u32[]{:S(2)}) collective-permute-start(f32[10,8,128]{2,1,0:T(8,128)S(1)} %get-tuple-element.26), channel_id=1, source_target_pairs={{0,1},{1,5},{2,3},{3,7},{4,0},{5,9},{6,2},{7,11},{8,4},{9,13},{10,... | collective-permute-start | bytes 122888 | tf_op jit(solution)/shard_map/ppermute | solution.py:256
  18.0 4.1 %collective-permute-start.5 = (f32[5,16,128]{2,1,0:T(8,128)S(1)}, f32[5,16,128]{2,1,0:T(8,128)S(1)}, u32[]{:S(2)}, u32[]{:S(2)}) collective-permute-start(f32[5,16,128]{2,1,0:T(8,128)S(1)} %get-tuple-element.25), channel_id=1, source_target_pairs={{0,1},{1,0},{2,3},{3,2},{4,5},{5,4},{6,7},{7,6},{8,9},{9,8},{10,11... | collective-permute-start | bytes 122888 | tf_op jit(solution)/shard_map/ppermute | solution.py:256
  19.1 4.2 %collective-permute-start.7 = (f32[5,8,128]{2,1,0:T(8,128)S(1)}, f32[5,8,128]{2,1,0:T(8,128)S(1)}, u32[]{:S(2)}, u32[]{:S(2)}) collective-permute-start(f32[5,8,128]{2,1,0:T(8,128)S(1)} %slice.8), channel_id=1, source_target_pairs={{0,1},{1,0},{2,3},{3,2},{4,5},{5,4},{6,7},{7,6},{8,9},{9,8},{10,11... | collective-permute-start | bytes 61448 | tf_op jit(solution)/shard_map/ppermute | solution.py:256

commit v3 on v1

--- a/solution.py
+++ b/solution.py
@@ -88,15 +88,14 @@
     lax.fori_loop(0, AGG, one_row, 0)
 
 
-def transpose_blocks(sources, place_ref, p_ref):
-    depth = place_ref.shape[1] * place_ref.shape[2] * place_ref.shape[3]
-    for side, (source, first) in enumerate(sources):
-        for pair in range(PAIRS):
-            for window in range(3):
-                place_ref[pair, window, side] = source[first + pair, window]
+def transpose_blocks(sources, p_ref):
     for pair in range(PAIRS):
-        turned = place_ref[pair].reshape(depth, 128).T
-        for place, part in enumerate(split_high_low(turned)):
+        block = jnp.concatenate(
+            [source[first + pair, window] for window in range(3) for source, first in sources],
+            axis=0,
+        )
+        depth = block.shape[0]
+        for place, part in enumerate(split_high_low(block.T)):
             for sub in range(2):
                 p_ref[2 * pair + sub, :, 128 * place : 128 * place + depth] = part[
                     64 * sub : 64 * sub + 64
@@ -114,19 +113,17 @@
         jnp.concatenate(blocks, axis=0),
         preferred_element_type=jnp.float32,
     )
-    return split_high_low(total[:, :128] + total[:, 128:])
-
-
-def stiff_kernel(mine, other, pair_both, k_ref, out_ref, place_ref, p_ref):
+    return jnp.concatenate(split_high_low(total[:, :128] + total[:, 128:]), axis=1)
+
+
+def stiff_kernel(mine, other, pair_both, k_ref, out_ref, p_ref):
     half = lax.axis_index("col") % 2
     for place, step, sources in (
         (0, 1, ((mine, 0), (pair_both, PAIRS))),
         (1, 2 - 2 * half, ((other, 0), (pair_both, 0))),
     ):
-        transpose_blocks(sources, place_ref.at[place], p_ref.at[place])
-        high, low = stiff_product(step, k_ref, p_ref.at[place])
-        out_ref[place, 0] = high
-        out_ref[place, 1] = low
+        transpose_blocks(sources, p_ref.at[place])
+        out_ref[place] = stiff_product(step, k_ref, p_ref.at[place])
 
 
 def coarse_terms(stiffs, pieces, windows, share, high_ref, low_ref):
@@ -158,10 +155,10 @@
     both = jnp.concatenate([high, low], axis=0)
     rows = len(windows) * width
     totals = []
-    for stiff_high, stiff_low in stiffs:
-        total = jnp.dot(both, stiff_high, preferred_element_type=jnp.float32)
-        rest = jnp.dot(high, stiff_low, preferred_element_type=jnp.float32)
-        totals.append(total[:rows] + total[rows:] + rest)
+    for stiff in stiffs:
+        total = jnp.dot(both, stiff, preferred_element_type=jnp.float32)
+        total = total[:rows] + total[rows:]
+        totals.append(total[:, :128] + total[:, 128:])
     mine, other, near = totals
     steps = (jnp.where(first_half, near, other), mine, jnp.where(first_half, other, near))
     terms = [[None] * 5 for _ in windows]
@@ -177,13 +174,12 @@
 
 def edge_kernel(count, share, k_ref, stiff, *refs):
     pieces = refs[:count]
-    near, pair_near, edge_ref, near_ref, place_ref, p_ref, high_ref, low_ref = refs[count:]
-    half = lax.axis_index("col") % 2
-    transpose_blocks(((near, 0), (pair_near, 0)), place_ref, p_ref)
-    high, low = stiff_product(2 * half, k_ref, p_ref)
-    near_ref[0] = high
-    near_ref[1] = low
-    stiffs = [(stiff[place, 0], stiff[place, 1]) for place in range(2)] + [(high, low)]
+    near, pair_near, edge_ref, near_ref, p_ref, high_ref, low_ref = refs[count:]
+    half = lax.axis_index("col") % 2
+    transpose_blocks(((near, 0), (pair_near, 0)), p_ref)
+    stiff_near = stiff_product(2 * half, k_ref, p_ref)
+    near_ref[...] = stiff_near
+    stiffs = [stiff[0], stiff[1], stiff_near]
     (terms,) = coarse_terms(stiffs, pieces, (2 * half,), share, high_ref, low_ref)
     for slot in range(5):
         for side in range(2):
@@ -197,8 +193,7 @@
     own_ref, pair_ref, high_ref, low_ref = refs[count:]
     half = lax.axis_index("col") % 2
     width = count * share
-    stiffs = [(stiff[place, 0], stiff[place, 1]) for place in range(2)]
-    stiffs.append((stiff_near[0], stiff_near[1]))
+    stiffs = [stiff[0], stiff[1], stiff_near[...]]
     windows = (1 - half, 2 - half)
     lower, upper = coarse_terms(stiffs, pieces, windows, share, high_ref, low_ref)
     for side, ref in ((0, own_ref), (1, pair_ref)):
@@ -311,18 +306,14 @@
     pieces[1] = pair_both
     pair_near = send(pair_both[:PAIRS], toward)
 
-    stiff_shape = (2, AGG * fine, 128)
-    place_shape = (PAIRS, 3, 2, padded, 128)
+    stiff_shape = (AGG * fine, 256)
     p_shape = (AGG, fine, 256)
     stiff = pl.pallas_call(
         stiff_kernel,
         out_shape=jax.ShapeDtypeStruct((2, *stiff_shape), jnp.bfloat16),
         in_specs=[vmem] * 4,
         out_specs=vmem,
-        scratch_shapes=[
-            pltpu.VMEM((2, *place_shape), jnp.float32),
-            pltpu.VMEM((2, *p_shape), jnp.bfloat16),
-        ],
+        scratch_shapes=[pltpu.VMEM((2, *p_shape), jnp.bfloat16)],
         compiler_params=params,
         cost_estimate=pl.CostEstimate(
             flops=1_000_000_000, bytes_accessed=3_000_000, transcendentals=0
@@ -341,7 +332,7 @@
         ],
         in_specs=[vmem] * (4 + cols_axis),
         out_specs=[vmem] * 2,
-        scratch_shapes=[pltpu.VMEM(place_shape, jnp.float32), pltpu.VMEM(p_shape, jnp.bfloat16)]
+        scratch_shapes=[pltpu.VMEM(p_shape, jnp.bfloat16)]
         + part_scratch(1),
         compiler_params=params,
         cost_estimate=pl.CostEstimate(

time: 24.5 us -> 24.4 us (level)
  no operation moved by 1% of the time
where the time goes in v3:
time: 24.4 us; the launch traced here: 24.2 us
  waiting for transfers between devices  9 us (37%)
  starting transfers between devices  8.48 us (35%)
  Pallas kernels  6.67 us (27%)
    ppermute x8, waiting for transfers between devices, send(): return lax.ppermute(value, ('row', 'col'), perm)  9 us
    ppermute x8, starting transfers between devices, send(): return lax.ppermute(value, ('row', 'col'), perm)  8.48 us
    pallas_call x1, Pallas kernels, body(): pl.pallas_call(functools.partial(split_kernel, slots, total_rows), out_sh...  2.28 us
    pallas_call x1, Pallas kernels, body(): pl.pallas_call(functools.partial(pack_kernel, blocks_all), out_shape=[bot...  1.18 us
    pallas_call x1, Pallas kernels, body(): pl.pallas_call(functools.partial(edge_kernel, cols_axis, padded), out_sha...  0.97 us
    pallas_call x1, Pallas kernels, body(): pl.pallas_call(functools.partial(sum_kernel, padded), out_shape=jax.Shape...  0.86 us
    pallas_call x1, Pallas kernels, body(): pl.pallas_call(stiff_kernel, out_shape=jax.ShapeDtypeStruct((2, *stiff_sh...  0.84 us
    pallas_call x1, Pallas kernels, body(): pl.pallas_call(functools.partial(inner_kernel, cols_axis, padded), out_sh...  0.55 us
  transfers between devices with their start and end apart: 8, of which 6 were waited for; matrix products, arithmetic and copies ran while one was open for 0% of the time, Pallas kernels for 15%

profile of v3, /device:TPU:0, one launch (start us, length us, event | category | flops | bytes accessed | tf_op | source)
XLA Modules:
  0.0 24.2 jit_solution(7589227865892127282)
XLA Ops:
  0.0 1.2 %pack_window.1 = (f32[8,3,16,128]{3,2,1,0:T(8,128)S(1)}, f32[4,3,16,128]{3,2,1,0:T(8,128)S(1)}, f32[4,3,16,128]{3,2,1,0:T(8,128)S(1)}, f32[4,3,16,128]{3,2,1,0:T(8,128)S(1)}, f32[4,3,16,128]{3,2,1,0:T(8,128)S(1)}) custom-call(s32[3,16]{1,0:T(4,128)} %bitcast.4, f32[16,3,16,64]{3,2,1,0:T(8,128)} %bitcast.3), custom_call_target="tpu_custom_call" | custom-call | tf_op jit(solution)/shard_map/pack_window/pallas_call | solution.py:268
  1.2 3.1 %collective-permute-start = (f32[8,3,16,128]{3,2,1,0:T(8,128)S(1)}, f32[8,3,16,128]{3,2,1,0:T(8,128)S(1)}, u32[]{:S(2)}, u32[]{:S(2)}) collective-permute-start(f32[8,3,16,128]{3,2,1,0:T(8,128)S(1)} %get-tuple-element.18), channel_id=1, source_target_pairs={{0,1},{1,0},{2,3},{3,2},{4,5},{5,4},{6,7},{7,6},{8,9},{9,8},{10,11... | collective-permute-start | bytes 589832 | tf_op jit(solution)/shard_map/ppermute | solution.py:251
  4.3 2.6 %collective-permute-start.1 = (f32[4,3,16,128]{3,2,1,0:T(8,128)S(1)}, f32[4,3,16,128]{3,2,1,0:T(8,128)S(1)}, u32[]{:S(2)}, u32[]{:S(2)}) collective-permute-start(f32[4,3,16,128]{3,2,1,0:T(8,128)S(1)} %get-tuple-element.21), channel_id=1, source_target_pairs={{0,2},{1,3},{2,0},{3,1},{4,6},{5,7},{6,4},{7,5},{8,10},{9,11},{10,... | collective-permute-start | bytes 294920 | tf_op jit(solution)/shard_map/ppermute | solution.py:251
  6.9 0.0 collective-permute-start.2
  6.9 0.0 collective-permute-start.3
  6.9 2.3 %split_stiffness.1.k_ref = bf16[8,25,64,128]{3,2,1,0:T(8,128)(2,1)S(1)} custom-call(s32[16,15]{1,0:T(8,128)} %cols_hbm.1, f32[16,15,64,64]{3,2,1,0:T(8,128)} %k_hbm.1), custom_call_target="tpu_custom_call" | custom-call | bytes 8000000 | tf_op jit(solution)/shard_map/split_stiffness/pallas_call | solution.py:289
  9.2 2.1 %collective-permute-done.pair_both.refs_1_ = f32[8,3,16,128]{3,2,1,0:T(8,128)S(1)} collective-permute-done((f32[8,3,16,128]{3,2,1,0:T(8,128)S(1)}, f32[8,3,16,128]{3,2,1,0:T(8,128)S(1)}, u32[]{:S(2)}, u32[]{:S(2)}) %collective-permute-start) | collective-permute-done | bytes 196640 | tf_op jit(solution)/shard_map/ppermute | solution.py:251
  11.3 0.1 collective-permute-start.4
  11.4 0.8 %stiff_prolong.1.stiff = bf16[2,512,256]{2,1,0:T(8,128)(2,1)S(1)} custom-call(f32[4,3,16,128]{3,2,1,0:T(8,128)S(1)} %get-tuple-element.16.mine.refs_0_, f32[4,3,16,128]{3,2,1,0:T(8,128)S(1)} %get-tuple-element.17.other, f32[8,3,16,128]{3,2,1,0:T(8,128)S(1)} %collective-permute-done.pair_both.refs_1_, bf16[8,25,64,128]{3,2,1,0:T(8,128)(2,1)S(1)} %split_stiffness.1.k_ref), custom_call_target="tpu_custom_call" | custom-call | flops 1000000000 | bytes 3000000 | tf_op jit(solution)/shard_map/stiff_prolong/pallas_call | solution.py:311
  12.2 0.0 collective-permute-done.1.refs_2_
  12.2 3.5 %collective-permute-done.2.refs_3_ = f32[4,3,16,128]{3,2,1,0:T(8,128)S(1)} collective-permute-done((f32[4,3,16,128]{3,2,1,0:T(8,128)S(1)}, f32[4,3,16,128]{3,2,1,0:T(8,128)S(1)}, u32[]{:S(2)}, u32[]{:S(2)}) %collective-permute-start.2) | collective-permute-done | bytes 98336 | tf_op jit(solution)/shard_map/ppermute | solution.py:251
  15.7 0.0 collective-permute-done.3.refs_4_
  15.7 0.6 %collective-permute-done.4.refs_5_ = f32[4,3,16,128]{3,2,1,0:T(8,128)S(1)} collective-permute-done((f32[4,3,16,128]{3,2,1,0:T(8,128)S(1)}, f32[4,3,16,128]{3,2,1,0:T(8,128)S(1)}, u32[]{:S(2)}, u32[]{:S(2)}) %collective-permute-start.4) | collective-permute-done | bytes 98336 | tf_op jit(solution)/shard_map/ppermute | solution.py:251
  16.3 1.0 %edge_terms.1 = (f32[10,8,128]{2,1,0:T(8,128)S(1)}, bf16[512,256]{1,0:T(8,128)(2,1)S(1)}) custom-call(bf16[8,25,64,128]{3,2,1,0:T(8,128)(2,1)S(1)} %split_stiffness.1.k_ref, bf16[2,512,256]{2,1,0:T(8,128)(2,1)S(1)} %stiff_prolong.1.stiff, f32[4,3,16,128]{3,2,1,0:T(8,128)S(1)} %get-tuple-element.16.mine.refs_0_, ...), custom_call_target="tpu_custom_call" | custom-call | flops 1000000000 | bytes 2000000 | tf_op jit(solution)/shard_map/edge_terms/pallas_call | solution.py:327
  17.3 0.3 %collective-permute-start.6 = (f32[10,8,128]{2,1,0:T(8,128)S(1)}, f32[10,8,128]{2,1,0:T(8,128)S(1)}, u32[]{:S(2)}, u32[]{:S(2)}) collective-permute-start(f32[10,8,128]{2,1,0:T(8,128)S(1)} %get-tuple-element.26), channel_id=1, source_target_pairs={{0,1},{1,5},{2,3},{3,7},{4,0},{5,9},{6,2},{7,11},{8,4},{9,13},{10,... | collective-permute-start | bytes 122888 | tf_op jit(solution)/shard_map/ppermute | solution.py:251
  17.6 0.5 %inner_terms.1 = (f32[5,16,128]{2,1,0:T(8,128)S(1)}, f32[5,16,128]{2,1,0:T(8,128)S(1)}) custom-call(bf16[2,512,256]{2,1,0:T(8,128)(2,1)S(1)} %stiff_prolong.1.stiff, bf16[512,256]{1,0:T(8,128)(2,1)S(1)} %get-tuple-element.23.stiff_near, f32[4,3,16,128]{3,2,1,0:T(8,128)S(1)} %get-tuple-element.16.mine.refs_0_, ...), custom_call_target="tpu_custom_call" | custom-call | flops 500000000 | bytes 1000000 | tf_op jit(solution)/shard_map/inner_terms/pallas_call | solution.py:346
  18.2 0.1 collective-permute-start.5
  18.2 1.0 %collective-permute-done.6.from_edge = f32[10,8,128]{2,1,0:T(8,128)S(1)} collective-permute-done((f32[10,8,128]{2,1,0:T(8,128)S(1)}, f32[10,8,128]{2,1,0:T(8,128)S(1)}, u32[]{:S(2)}, u32[]{:S(2)}) %collective-permute-start.6) | collective-permute-done | bytes 40992 | tf_op jit(solution)/shard_map/ppermute | solution.py:251
  19.3 2.3 %collective-permute-start.7 = (f32[5,8,128]{2,1,0:T(8,128)S(1)}, f32[5,8,128]{2,1,0:T(8,128)S(1)}, u32[]{:S(2)}, u32[]{:S(2)}) collective-permute-start(f32[5,8,128]{2,1,0:T(8,128)S(1)} %slice.8), channel_id=1, source_target_pairs={{0,1},{1,0},{2,3},{3,2},{4,5},{5,4},{6,7},{7,6},{8,9},{9,8},{10,11... | collective-permute-start | bytes 61448 | tf_op jit(solution)/shard_map/ppermute | solution.py:251
  21.6 0.6 %collective-permute-done.5.from_pair = f32[5,16,128]{2,1,0:T(8,128)S(1)} collective-permute-done((f32[5,16,128]{2,1,0:T(8,128)S(1)}, f32[5,16,128]{2,1,0:T(8,128)S(1)}, u32[]{:S(2)}, u32[]{:S(2)}) %collective-permute-start.5) | collective-permute-done | bytes 40992 | tf_op jit(solution)/shard_map/ppermute | solution.py:251
  22.2 1.1 %collective-permute-done.7.from_pair_edge = f32[5,8,128]{2,1,0:T(8,128)S(1)} collective-permute-done((f32[5,8,128]{2,1,0:T(8,128)S(1)}, f32[5,8,128]{2,1,0:T(8,128)S(1)}, u32[]{:S(2)}, u32[]{:S(2)}) %collective-permute-start.7) | collective-permute-done | bytes 20512 | tf_op jit(solution)/shard_map/ppermute | solution.py:251
  23.4 0.9 %sum_terms.1 = f32[2,7,16,64]{3,2,1,0:T(8,128)} custom-call(f32[5,16,128]{2,1,0:T(8,128)S(1)} %get-tuple-element.24.own, f32[5,16,128]{2,1,0:T(8,128)S(1)} %collective-permute-done.5.from_pair, f32[10,8,128]{2,1,0:T(8,128)S(1)} %collective-permute-done.6.from_edge, f32[5,8,128]{2,1,0:T(8,128)S(1)} %collective-permute-done.7.from_pair_edge), custom_call_target="tpu_custom_call" | custom-call | tf_op jit(solution)/shard_map/sum_terms/pallas_call | solution.py:361
  (2 shorter events, 0.0 us)
Async XLA Ops:
  1.2 10.1 %collective-permute-start = (f32[8,3,16,128]{3,2,1,0:T(8,128)S(1)}, f32[8,3,16,128]{3,2,1,0:T(8,128)S(1)}, u32[]{:S(2)}, u32[]{:S(2)}) collective-permute-start(f32[8,3,16,128]{3,2,1,0:T(8,128)S(1)} %get-tuple-element.18), channel_id=1, source_target_pairs={{0,1},{1,0},{2,3},{3,2},{4,5},{5,4},{6,7},{7,6},{8,9},{9,8},{10,11... | collective-permute-start | bytes 589832 | tf_op jit(solution)/shard_map/ppermute | solution.py:251
  4.3 7.9 %collective-permute-start.1 = (f32[4,3,16,128]{3,2,1,0:T(8,128)S(1)}, f32[4,3,16,128]{3,2,1,0:T(8,128)S(1)}, u32[]{:S(2)}, u32[]{:S(2)}) collective-permute-start(f32[4,3,16,128]{3,2,1,0:T(8,128)S(1)} %get-tuple-element.21), channel_id=1, source_target_pairs={{0,2},{1,3},{2,0},{3,1},{4,6},{5,7},{6,4},{7,5},{8,10},{9,11},{10,... | collective-permute-start | bytes 294920 | tf_op jit(solution)/shard_map/ppermute | solution.py:251
  6.9 8.8 %collective-permute-start.2 = (f32[4,3,16,128]{3,2,1,0:T(8,128)S(1)}, f32[4,3,16,128]{3,2,1,0:T(8,128)S(1)}, u32[]{:S(2)}, u32[]{:S(2)}) collective-permute-start(f32[4,3,16,128]{3,2,1,0:T(8,128)S(1)} %get-tuple-element.22), channel_id=1, source_target_pairs={{0,3},{1,2},{2,1},{3,0},{4,7},{5,6},{6,5},{7,4},{8,11},{9,10},{10,... | collective-permute-start | bytes 294920 | tf_op jit(solution)/shard_map/ppermute | solution.py:251
  6.9 8.8 %collective-permute-start.3 = (f32[4,3,16,128]{3,2,1,0:T(8,128)S(1)}, f32[4,3,16,128]{3,2,1,0:T(8,128)S(1)}, u32[]{:S(2)}, u32[]{:S(2)}) collective-permute-start(f32[4,3,16,128]{3,2,1,0:T(8,128)S(1)} %get-tuple-element.17.other), channel_id=1, source_target_pairs={{0,4},{1,29},{2,6},{3,31},{4,8},{5,1},{6,10},{7,3},{8,12},{9,5},{1... | collective-permute-start | bytes 294920 | tf_op jit(solution)/shard_map/ppermute | solution.py:251
  11.3 5.0 %collective-permute-start.4 = (f32[4,3,16,128]{3,2,1,0:T(8,128)S(1)}, f32[4,3,16,128]{3,2,1,0:T(8,128)S(1)}, u32[]{:S(2)}, u32[]{:S(2)}) collective-permute-start(f32[4,3,16,128]{3,2,1,0:T(8,128)S(1)} %slice.6), channel_id=1, source_target_pairs={{0,4},{1,29},{2,6},{3,31},{4,8},{5,1},{6,10},{7,3},{8,12},{9,5},{1... | collective-permute-start | bytes 294920 | tf_op jit(solution)/shard_map/ppermute | solution.py:251
  17.3 2.0 %collective-permute-start.6 = (f32[10,8,128]{2,1,0:T(8,128)S(1)}, f32[10,8,128]{2,1,0:T(8,128)S(1)}, u32[]{:S(2)}, u32[]{:S(2)}) collective-permute-start(f32[10,8,128]{2,1,0:T(8,128)S(1)} %get-tuple-element.26), channel_id=1, source_target_pairs={{0,1},{1,5},{2,3},{3,7},{4,0},{5,9},{6,2},{7,11},{8,4},{9,13},{10,... | collective-permute-start | bytes 122888 | tf_op jit(solution)/shard_map/ppermute | solution.py:251
  18.2 4.1 %collective-permute-start.5 = (f32[5,16,128]{2,1,0:T(8,128)S(1)}, f32[5,16,128]{2,1,0:T(8,128)S(1)}, u32[]{:S(2)}, u32[]{:S(2)}) collective-permute-start(f32[5,16,128]{2,1,0:T(8,128)S(1)} %get-tuple-element.25), channel_id=1, source_target_pairs={{0,1},{1,0},{2,3},{3,2},{4,5},{5,4},{6,7},{7,6},{8,9},{9,8},{10,11... | collective-permute-start | bytes 122888 | tf_op jit(solution)/shard_map/ppermute | solution.py:251
  19.3 4.1 %collective-permute-start.7 = (f32[5,8,128]{2,1,0:T(8,128)S(1)}, f32[5,8,128]{2,1,0:T(8,128)S(1)}, u32[]{:S(2)}, u32[]{:S(2)}) collective-permute-start(f32[5,8,128]{2,1,0:T(8,128)S(1)} %slice.8), channel_id=1, source_target_pairs={{0,1},{1,0},{2,3},{3,2},{4,5},{5,4},{6,7},{7,6},{8,9},{9,8},{10,11... | collective-permute-start | bytes 61448 | tf_op jit(solution)/shard_map/ppermute | solution.py:251

commit v4 on v3

--- a/solution.py
+++ b/solution.py
@@ -18,7 +18,7 @@
 
 
 def pack_kernel(
-    blocks_all, cols_hbm, p_hbm, both_ref, mine_ref, other_ref, mine_again, other_again,
+    blocks_all, cols_hbm, p_hbm, mine_ref, other_ref, mine_again, other_again,
     cols_ref, p_ref, sems,
 ):
     cols_copy = pltpu.make_async_copy(cols_hbm, cols_ref, sems.at[0])
@@ -51,7 +51,6 @@
                 packed = jnp.concatenate(halves, axis=1)
                 out_ref[pair, window] = packed
                 again[pair, window] = packed
-                both_ref[part * PAIRS + pair, window] = packed
 
 
 def split_kernel(slots, total_rows, cols_hbm, k_hbm, out_ref, cols_ref, k_ref, cols_sem, sems):
@@ -91,7 +90,7 @@
 def transpose_blocks(sources, p_ref):
     for pair in range(PAIRS):
         block = jnp.concatenate(
-            [source[first + pair, window] for window in range(3) for source, first in sources],
+            [source[pair, window] for window in range(3) for source in sources],
             axis=0,
         )
         depth = block.shape[0]
@@ -116,14 +115,10 @@
     return jnp.concatenate(split_high_low(total[:, :128] + total[:, 128:]), axis=1)
 
 
-def stiff_kernel(mine, other, pair_both, k_ref, out_ref, p_ref):
-    half = lax.axis_index("col") % 2
-    for place, step, sources in (
-        (0, 1, ((mine, 0), (pair_both, PAIRS))),
-        (1, 2 - 2 * half, ((other, 0), (pair_both, 0))),
-    ):
-        transpose_blocks(sources, p_ref.at[place])
-        out_ref[place] = stiff_product(step, k_ref, p_ref.at[place])
+def stiff_kernel(other, pair_other, k_ref, out_ref, p_ref):
+    half = lax.axis_index("col") % 2
+    transpose_blocks((other, pair_other), p_ref)
+    out_ref[...] = stiff_product(2 - 2 * half, k_ref, p_ref)
 
 
 def coarse_terms(stiffs, pieces, windows, share, high_ref, low_ref):
@@ -134,9 +129,8 @@
     first_half = position % 2 == 0
     for place, window in enumerate(windows):
         for shift in range(count):
-            first = PAIRS if shift == 1 else 0
             for pair in range(PAIRS):
-                high, low = split_high_low(pieces[shift][first + pair, window])
+                high, low = split_high_low(pieces[shift][pair, window])
                 high_ref[place, pair, position ^ shift] = high
                 low_ref[place, pair, position ^ shift] = low
 
@@ -172,14 +166,22 @@
     return terms
 
 
-def edge_kernel(count, share, k_ref, stiff, *refs):
-    pieces = refs[:count]
-    near, pair_near, edge_ref, near_ref, p_ref, high_ref, low_ref = refs[count:]
-    half = lax.axis_index("col") % 2
-    transpose_blocks(((near, 0), (pair_near, 0)), p_ref)
-    stiff_near = stiff_product(2 * half, k_ref, p_ref)
-    near_ref[...] = stiff_near
-    stiffs = [stiff[0], stiff[1], stiff_near]
+def edge_kernel(count, share, k_ref, stiff_other, *refs):
+    mine = refs[0]
+    far = refs[1 : count - 1]
+    near, pair_near, pair_mine = refs[count - 1 : count + 2]
+    edge_ref, stiff_ref, p_ref, high_ref, low_ref = refs[count + 2 :]
+    half = lax.axis_index("col") % 2
+    stiffs = []
+    for place, step, sources in (
+        (0, 1, (mine, pair_mine)),
+        (1, 2 * half, (near, pair_near)),
+    ):
+        transpose_blocks(sources, p_ref.at[place])
+        stiffs.append(stiff_product(step, k_ref, p_ref.at[place]))
+        stiff_ref[place] = stiffs[place]
+    stiffs.insert(1, stiff_other[...])
+    pieces = [mine, pair_mine, *far]
     (terms,) = coarse_terms(stiffs, pieces, (2 * half,), share, high_ref, low_ref)
     for slot in range(5):
         for side in range(2):
@@ -188,12 +190,12 @@
             edge_ref[5 * side + slot] = folded
 
 
-def inner_kernel(count, share, stiff, stiff_near, *refs):
+def inner_kernel(count, share, stiff_other, stiff, *refs):
     pieces = refs[:count]
     own_ref, pair_ref, high_ref, low_ref = refs[count:]
     half = lax.axis_index("col") % 2
     width = count * share
-    stiffs = [stiff[0], stiff[1], stiff_near[...]]
+    stiffs = [stiff[0], stiff_other[...], stiff[1]]
     windows = (1 - half, 2 - half)
     lower, upper = coarse_terms(stiffs, pieces, windows, share, high_ref, low_ref)
     for side, ref in ((0, own_ref), (1, pair_ref)):
@@ -264,12 +266,11 @@
     if padded != share:
         p_rows = jnp.pad(p_rows, ((0, 0), (0, 0), (0, padded - share), (0, 0)))
     group_shape = jax.ShapeDtypeStruct((PAIRS, 3, padded, 128), jnp.float32)
-    both_shape = jax.ShapeDtypeStruct((2 * PAIRS, 3, padded, 128), jnp.float32)
-    both, mine, other, mine_again, other_again = pl.pallas_call(
+    mine, other, mine_again, other_again = pl.pallas_call(
         functools.partial(pack_kernel, blocks_all),
-        out_shape=[both_shape] + [group_shape] * 4,
+        out_shape=[group_shape] * 4,
         in_specs=[hbm, hbm],
-        out_specs=[vmem] * 5,
+        out_specs=[vmem] * 4,
         scratch_shapes=[
             pltpu.SMEM(p_cols.T.shape, jnp.int32),
             pltpu.VMEM(p_rows.shape, jnp.float32),
@@ -279,10 +280,10 @@
         name="pack_window",
     )(in_hbm(p_cols.T), in_hbm(p_rows))
 
-    pair_both = send(both, swap)
-    pieces = [mine, pair_both]
+    pair_other = send(mine, swap)
+    far = []
     for shift in range(2, cols_axis):
-        pieces.append(
+        far.append(
             send(mine_again if shift % 2 == 0 else other_again, lambda row, col: (row, col ^ shift))
         )
     near = send(other, toward)
@@ -302,44 +303,44 @@
         name="split_stiffness",
     )(in_hbm(k_cols), in_hbm(k_vals))
 
-    k_split, pair_both = lax.optimization_barrier((k_split, pair_both))
-    pieces[1] = pair_both
-    pair_near = send(pair_both[:PAIRS], toward)
+    k_split, pair_other, other_late = lax.optimization_barrier((k_split, pair_other, other))
+    pair_near = send(pair_other, toward)
+    pair_mine = send(other_late, swap)
+    pieces = [mine, pair_mine, *far]
 
     stiff_shape = (AGG * fine, 256)
     p_shape = (AGG, fine, 256)
-    stiff = pl.pallas_call(
+    stiff_other = pl.pallas_call(
         stiff_kernel,
-        out_shape=jax.ShapeDtypeStruct((2, *stiff_shape), jnp.bfloat16),
-        in_specs=[vmem] * 4,
+        out_shape=jax.ShapeDtypeStruct(stiff_shape, jnp.bfloat16),
+        in_specs=[vmem] * 3,
         out_specs=vmem,
-        scratch_shapes=[pltpu.VMEM((2, *p_shape), jnp.bfloat16)],
+        scratch_shapes=[pltpu.VMEM(p_shape, jnp.bfloat16)],
         compiler_params=params,
         cost_estimate=pl.CostEstimate(
-            flops=1_000_000_000, bytes_accessed=3_000_000, transcendentals=0
+            flops=500_000_000, bytes_accessed=1_000_000, transcendentals=0
         ),
         name="stiff_prolong",
-    )(mine, other, pair_both, k_split)
+    )(other, pair_other, k_split)
 
     def part_scratch(windows):
         return [pltpu.VMEM((windows, PAIRS, cols_axis, padded, 128), jnp.bfloat16)] * 2
 
-    edge, stiff_near = pl.pallas_call(
+    edge, stiff = pl.pallas_call(
         functools.partial(edge_kernel, cols_axis, padded),
         out_shape=[
             jax.ShapeDtypeStruct((10, padded // 2, 2 * width), jnp.float32),
-            jax.ShapeDtypeStruct(stiff_shape, jnp.bfloat16),
+            jax.ShapeDtypeStruct((2, *stiff_shape), jnp.bfloat16),
         ],
         in_specs=[vmem] * (4 + cols_axis),
         out_specs=[vmem] * 2,
-        scratch_shapes=[pltpu.VMEM(p_shape, jnp.bfloat16)]
-        + part_scratch(1),
+        scratch_shapes=[pltpu.VMEM((2, *p_shape), jnp.bfloat16)] + part_scratch(1),
         compiler_params=params,
         cost_estimate=pl.CostEstimate(
             flops=1_000_000_000, bytes_accessed=2_000_000, transcendentals=0
         ),
         name="edge_terms",
-    )(k_split, stiff, *pieces, near, pair_near)
+    )(k_split, stiff_other, mine, *far, near, pair_near, pair_mine)
     from_edge = send(edge, away)
 
     band_shape = jax.ShapeDtypeStruct((5, padded, 2 * width), jnp.float32)
@@ -354,7 +355,7 @@
             flops=500_000_000, bytes_accessed=1_000_000, transcendentals=0
         ),
         name="inner_terms",
-    )(stiff, stiff_near, *pieces)
+    )(stiff_other, stiff, *pieces)
     from_pair = send(for_pair, swap)
     from_pair_edge = send(from_edge[5:], swap)
 

time: 24.4 us -> 24.4 us (level)
  starting transfers between devices: 8.48 us -> 10.8 us
  waiting for transfers between devices: 9 us -> 6.73 us
    ppermute x8 -> x9, starting transfers between devices: 8.48 us -> 10.8 us  [send(): return lax.ppermute(value, ('row', 'col'), perm)]
    ppermute x8 -> x9, waiting for transfers between devices: 9 us -> 6.73 us  [send(): return lax.ppermute(value, ('row', 'col'), perm)]
    pallas_call x2, Pallas kernels: 2.02 us -> 1.73 us  [the longest x1 1.18 us: body(): pl.pallas_call(functools.partial(pack_kernel, blocks_all), out_shape=[gro...]
  transfers between devices with their start and end apart: 8 -> 9, of which waited for: 6 -> 5; matrix products, arithmetic and copies ran while one was open for 0% -> 0% of each run, Pallas kernels for 15% -> 14%
where the time goes in v4:
time: 24.4 us; the launch traced here: 24.2 us
  starting transfers between devices  10.8 us (44%)
  waiting for transfers between devices  6.73 us (28%)
  Pallas kernels  6.61 us (27%)
    ppermute x9, starting transfers between devices, send(): return lax.ppermute(value, ('row', 'col'), perm)  10.8 us
    ppermute x9, waiting for transfers between devices, send(): return lax.ppermute(value, ('row', 'col'), perm)  6.73 us
    pallas_call x1, Pallas kernels, body(): pl.pallas_call(functools.partial(split_kernel, slots, total_rows), out_sh...  2.28 us
    pallas_call x1, Pallas kernels, body(): pl.pallas_call(functools.partial(edge_kernel, cols_axis, padded), out_sha...  1.2 us
    pallas_call x1, Pallas kernels, body(): pl.pallas_call(functools.partial(pack_kernel, blocks_all), out_shape=[gro...  1.18 us
    pallas_call x1, Pallas kernels, body(): pl.pallas_call(functools.partial(sum_kernel, padded), out_shape=jax.Shape...  0.86 us
    pallas_call x1, Pallas kernels, body(): pl.pallas_call(stiff_kernel, out_shape=jax.ShapeDtypeStruct(stiff_shape,...  0.55 us
    pallas_call x1, Pallas kernels, body(): pl.pallas_call(functools.partial(inner_kernel, cols_axis, padded), out_sh...  0.55 us
  transfers between devices with their start and end apart: 9, of which 5 were waited for; matrix products, arithmetic and copies ran while one was open for 0% of the time, Pallas kernels for 14%

profile of v4, /device:TPU:0, one launch (start us, length us, event | category | flops | bytes accessed | tf_op | source)
XLA Modules:
  0.0 24.2 jit_solution(15599118937329790223)
XLA Ops:
  0.0 1.2 %pack_window.1 = (f32[4,3,16,128]{3,2,1,0:T(8,128)S(1)}, f32[4,3,16,128]{3,2,1,0:T(8,128)S(1)}, f32[4,3,16,128]{3,2,1,0:T(8,128)S(1)}, f32[4,3,16,128]{3,2,1,0:T(8,128)S(1)}) custom-call(s32[3,16]{1,0:T(4,128)} %bitcast.4, f32[16,3,16,64]{3,2,1,0:T(8,128)} %bitcast.3), custom_call_target="tpu_custom_call" | custom-call | tf_op jit(solution)/shard_map/pack_window/pallas_call | solution.py:269
  1.2 3.1 %collective-permute-start = (f32[4,3,16,128]{3,2,1,0:T(8,128)S(1)}, f32[4,3,16,128]{3,2,1,0:T(8,128)S(1)}, u32[]{:S(2)}, u32[]{:S(2)}) collective-permute-start(f32[4,3,16,128]{3,2,1,0:T(8,128)S(1)} %get-tuple-element.17.refs_0_), channel_id=1, source_target_pairs={{0,1},{1,0},{2,3},{3,2},{4,5},{5,4},{6,7},{7,6},{8,9},{9,8},{10,11... | collective-permute-start | bytes 294920 | tf_op jit(solution)/shard_map/ppermute | solution.py:253
  4.3 2.6 %collective-permute-start.1 = (f32[4,3,16,128]{3,2,1,0:T(8,128)S(1)}, f32[4,3,16,128]{3,2,1,0:T(8,128)S(1)}, u32[]{:S(2)}, u32[]{:S(2)}) collective-permute-start(f32[4,3,16,128]{3,2,1,0:T(8,128)S(1)} %get-tuple-element.20), channel_id=1, source_target_pairs={{0,2},{1,3},{2,0},{3,1},{4,6},{5,7},{6,4},{7,5},{8,10},{9,11},{10,... | collective-permute-start | bytes 294920 | tf_op jit(solution)/shard_map/ppermute | solution.py:253
  6.9 0.0 collective-permute-start.2
  6.9 0.0 collective-permute-start.3
  6.9 2.3 %split_stiffness.1.k_ref = bf16[8,25,64,128]{3,2,1,0:T(8,128)(2,1)S(1)} custom-call(s32[16,15]{1,0:T(8,128)} %cols_hbm.1, f32[16,15,64,64]{3,2,1,0:T(8,128)} %k_hbm.1), custom_call_target="tpu_custom_call" | custom-call | bytes 8000000 | tf_op jit(solution)/shard_map/split_stiffness/pallas_call | solution.py:290
  9.2 0.0 collective-permute-done.pair_other
  9.2 2.0 %collective-permute-start.5 = (f32[4,3,16,128]{3,2,1,0:T(8,128)S(1)}, f32[4,3,16,128]{3,2,1,0:T(8,128)S(1)}, u32[]{:S(2)}, u32[]{:S(2)}) collective-permute-start(f32[4,3,16,128]{3,2,1,0:T(8,128)S(1)} %get-tuple-element.22.other), channel_id=1, source_target_pairs={{0,1},{1,0},{2,3},{3,2},{4,5},{5,4},{6,7},{7,6},{8,9},{9,8},{10,11... | collective-permute-start | bytes 294920 | tf_op jit(solution)/shard_map/ppermute | solution.py:253
  11.2 0.0 collective-permute-start.4
  11.2 0.5 %stiff_prolong.1.stiff_other = bf16[512,256]{1,0:T(8,128)(2,1)S(1)} custom-call(f32[4,3,16,128]{3,2,1,0:T(8,128)S(1)} %get-tuple-element.22.other, f32[4,3,16,128]{3,2,1,0:T(8,128)S(1)} %collective-permute-done.pair_other, bf16[8,25,64,128]{3,2,1,0:T(8,128)(2,1)S(1)} %split_stiffness.1.k_ref), custom_call_target="tpu_custom_call" | custom-call | flops 500000000 | bytes 1000000 | tf_op jit(solution)/shard_map/stiff_prolong/pallas_call | solution.py:313
  11.7 3.0 %collective-permute-done.1.refs_1_.refs_2_ = f32[4,3,16,128]{3,2,1,0:T(8,128)S(1)} collective-permute-done((f32[4,3,16,128]{3,2,1,0:T(8,128)S(1)}, f32[4,3,16,128]{3,2,1,0:T(8,128)S(1)}, u32[]{:S(2)}, u32[]{:S(2)}) %collective-permute-start.1) | collective-permute-done | bytes 98336 | tf_op jit(solution)/shard_map/ppermute | solution.py:253
  14.7 0.0 collective-permute-done.2.refs_2_.refs_3_
  14.7 0.0 collective-permute-done.3.refs_3_
  14.7 1.4 %collective-permute-done.5.refs_5_.refs_1_ = f32[4,3,16,128]{3,2,1,0:T(8,128)S(1)} collective-permute-done((f32[4,3,16,128]{3,2,1,0:T(8,128)S(1)}, f32[4,3,16,128]{3,2,1,0:T(8,128)S(1)}, u32[]{:S(2)}, u32[]{:S(2)}) %collective-permute-start.5) | collective-permute-done | bytes 98336 | tf_op jit(solution)/shard_map/ppermute | solution.py:253
  16.2 0.0 collective-permute-done.4.refs_4_
  16.2 1.2 %edge_terms.1 = (f32[10,8,128]{2,1,0:T(8,128)S(1)}, bf16[2,512,256]{2,1,0:T(8,128)(2,1)S(1)}) custom-call(bf16[8,25,64,128]{3,2,1,0:T(8,128)(2,1)S(1)} %split_stiffness.1.k_ref, bf16[512,256]{1,0:T(8,128)(2,1)S(1)} %stiff_prolong.1.stiff_other, f32[4,3,16,128]{3,2,1,0:T(8,128)S(1)} %get-tuple-element.17.refs_0_, ...), custom_call_target="tpu_custom_call" | custom-call | flops 1000000000 | bytes 2000000 | tf_op jit(solution)/shard_map/edge_terms/pallas_call | solution.py:329
  17.4 0.2 collective-permute-start.7
  17.6 0.5 %inner_terms.1 = (f32[5,16,128]{2,1,0:T(8,128)S(1)}, f32[5,16,128]{2,1,0:T(8,128)S(1)}) custom-call(bf16[512,256]{1,0:T(8,128)(2,1)S(1)} %stiff_prolong.1.stiff_other, bf16[2,512,256]{2,1,0:T(8,128)(2,1)S(1)} %get-tuple-element.23.stiff, f32[4,3,16,128]{3,2,1,0:T(8,128)S(1)} %get-tuple-element.17.refs_0_, ...), custom_call_target="tpu_custom_call" | custom-call | flops 500000000 | bytes 1000000 | tf_op jit(solution)/shard_map/inner_terms/pallas_call | solution.py:347
  18.2 0.6 %collective-permute-start.6 = (f32[5,16,128]{2,1,0:T(8,128)S(1)}, f32[5,16,128]{2,1,0:T(8,128)S(1)}, u32[]{:S(2)}, u32[]{:S(2)}) collective-permute-start(f32[5,16,128]{2,1,0:T(8,128)S(1)} %get-tuple-element.25), channel_id=1, source_target_pairs={{0,1},{1,0},{2,3},{3,2},{4,5},{5,4},{6,7},{7,6},{8,9},{9,8},{10,11... | collective-permute-start | bytes 122888 | tf_op jit(solution)/shard_map/ppermute | solution.py:253
  18.7 0.5 %collective-permute-done.7.from_edge = f32[10,8,128]{2,1,0:T(8,128)S(1)} collective-permute-done((f32[10,8,128]{2,1,0:T(8,128)S(1)}, f32[10,8,128]{2,1,0:T(8,128)S(1)}, u32[]{:S(2)}, u32[]{:S(2)}) %collective-permute-start.7) | collective-permute-done | bytes 40992 | tf_op jit(solution)/shard_map/ppermute | solution.py:253
  19.3 2.3 %collective-permute-start.8 = (f32[5,8,128]{2,1,0:T(8,128)S(1)}, f32[5,8,128]{2,1,0:T(8,128)S(1)}, u32[]{:S(2)}, u32[]{:S(2)}) collective-permute-start(f32[5,8,128]{2,1,0:T(8,128)S(1)} %slice.4), channel_id=1, source_target_pairs={{0,1},{1,0},{2,3},{3,2},{4,5},{5,4},{6,7},{7,6},{8,9},{9,8},{10,11... | collective-permute-start | bytes 61448 | tf_op jit(solution)/shard_map/ppermute | solution.py:253
  21.6 0.6 %collective-permute-done.6.from_pair = f32[5,16,128]{2,1,0:T(8,128)S(1)} collective-permute-done((f32[5,16,128]{2,1,0:T(8,128)S(1)}, f32[5,16,128]{2,1,0:T(8,128)S(1)}, u32[]{:S(2)}, u32[]{:S(2)}) %collective-permute-start.6) | collective-permute-done | bytes 40992 | tf_op jit(solution)/shard_map/ppermute | solution.py:253
  22.2 1.1 %collective-permute-done.8.from_pair_edge = f32[5,8,128]{2,1,0:T(8,128)S(1)} collective-permute-done((f32[5,8,128]{2,1,0:T(8,128)S(1)}, f32[5,8,128]{2,1,0:T(8,128)S(1)}, u32[]{:S(2)}, u32[]{:S(2)}) %collective-permute-start.8) | collective-permute-done | bytes 20512 | tf_op jit(solution)/shard_map/ppermute | solution.py:253
  23.4 0.9 %sum_terms.1 = f32[2,7,16,64]{3,2,1,0:T(8,128)} custom-call(f32[5,16,128]{2,1,0:T(8,128)S(1)} %get-tuple-element.24.own, f32[5,16,128]{2,1,0:T(8,128)S(1)} %collective-permute-done.6.from_pair, f32[10,8,128]{2,1,0:T(8,128)S(1)} %collective-permute-done.7.from_edge, f32[5,8,128]{2,1,0:T(8,128)S(1)} %collective-permute-done.8.from_pair_edge), custom_call_target="tpu_custom_call" | custom-call | tf_op jit(solution)/shard_map/sum_terms/pallas_call | solution.py:362
  (1 shorter events, 0.0 us)
Async XLA Ops:
  1.2 8.0 %collective-permute-start = (f32[4,3,16,128]{3,2,1,0:T(8,128)S(1)}, f32[4,3,16,128]{3,2,1,0:T(8,128)S(1)}, u32[]{:S(2)}, u32[]{:S(2)}) collective-permute-start(f32[4,3,16,128]{3,2,1,0:T(8,128)S(1)} %get-tuple-element.17.refs_0_), channel_id=1, source_target_pairs={{0,1},{1,0},{2,3},{3,2},{4,5},{5,4},{6,7},{7,6},{8,9},{9,8},{10,11... | collective-permute-start | bytes 294920 | tf_op jit(solution)/shard_map/ppermute | solution.py:253
  4.3 10.4 %collective-permute-start.1 = (f32[4,3,16,128]{3,2,1,0:T(8,128)S(1)}, f32[4,3,16,128]{3,2,1,0:T(8,128)S(1)}, u32[]{:S(2)}, u32[]{:S(2)}) collective-permute-start(f32[4,3,16,128]{3,2,1,0:T(8,128)S(1)} %get-tuple-element.20), channel_id=1, source_target_pairs={{0,2},{1,3},{2,0},{3,1},{4,6},{5,7},{6,4},{7,5},{8,10},{9,11},{10,... | collective-permute-start | bytes 294920 | tf_op jit(solution)/shard_map/ppermute | solution.py:253
  6.9 7.8 %collective-permute-start.2 = (f32[4,3,16,128]{3,2,1,0:T(8,128)S(1)}, f32[4,3,16,128]{3,2,1,0:T(8,128)S(1)}, u32[]{:S(2)}, u32[]{:S(2)}) collective-permute-start(f32[4,3,16,128]{3,2,1,0:T(8,128)S(1)} %get-tuple-element.21), channel_id=1, source_target_pairs={{0,3},{1,2},{2,1},{3,0},{4,7},{5,6},{6,5},{7,4},{8,11},{9,10},{10,... | collective-permute-start | bytes 294920 | tf_op jit(solution)/shard_map/ppermute | solution.py:253
  6.9 7.8 %collective-permute-start.3 = (f32[4,3,16,128]{3,2,1,0:T(8,128)S(1)}, f32[4,3,16,128]{3,2,1,0:T(8,128)S(1)}, u32[]{:S(2)}, u32[]{:S(2)}) collective-permute-start(f32[4,3,16,128]{3,2,1,0:T(8,128)S(1)} %get-tuple-element.22.other), channel_id=1, source_target_pairs={{0,4},{1,29},{2,6},{3,31},{4,8},{5,1},{6,10},{7,3},{8,12},{9,5},{1... | collective-permute-start | bytes 294920 | tf_op jit(solution)/shard_map/ppermute | solution.py:253
  9.2 7.0 %collective-permute-start.5 = (f32[4,3,16,128]{3,2,1,0:T(8,128)S(1)}, f32[4,3,16,128]{3,2,1,0:T(8,128)S(1)}, u32[]{:S(2)}, u32[]{:S(2)}) collective-permute-start(f32[4,3,16,128]{3,2,1,0:T(8,128)S(1)} %get-tuple-element.22.other), channel_id=1, source_target_pairs={{0,1},{1,0},{2,3},{3,2},{4,5},{5,4},{6,7},{7,6},{8,9},{9,8},{10,11... | collective-permute-start | bytes 294920 | tf_op jit(solution)/shard_map/ppermute | solution.py:253
  11.2 5.0 %collective-permute-start.4 = (f32[4,3,16,128]{3,2,1,0:T(8,128)S(1)}, f32[4,3,16,128]{3,2,1,0:T(8,128)S(1)}, u32[]{:S(2)}, u32[]{:S(2)}) collective-permute-start(f32[4,3,16,128]{3,2,1,0:T(8,128)S(1)} %collective-permute-done.pair_other), channel_id=1, source_target_pairs={{0,4},{1,29},{2,6},{3,31},{4,8},{5,1},{6,10},{7,3},{8,12},{9,5},{1... | collective-permute-start | bytes 294920 | tf_op jit(solution)/shard_map/ppermute | solution.py:253
  17.4 1.9 %collective-permute-start.7 = (f32[10,8,128]{2,1,0:T(8,128)S(1)}, f32[10,8,128]{2,1,0:T(8,128)S(1)}, u32[]{:S(2)}, u32[]{:S(2)}) collective-permute-start(f32[10,8,128]{2,1,0:T(8,128)S(1)} %get-tuple-element.26), channel_id=1, source_target_pairs={{0,1},{1,5},{2,3},{3,7},{4,0},{5,9},{6,2},{7,11},{8,4},{9,13},{10,... | collective-permute-start | bytes 122888 | tf_op jit(solution)/shard_map/ppermute | solution.py:253
  18.2 4.1 %collective-permute-start.6 = (f32[5,16,128]{2,1,0:T(8,128)S(1)}, f32[5,16,128]{2,1,0:T(8,128)S(1)}, u32[]{:S(2)}, u32[]{:S(2)}) collective-permute-start(f32[5,16,128]{2,1,0:T(8,128)S(1)} %get-tuple-element.25), channel_id=1, source_target_pairs={{0,1},{1,0},{2,3},{3,2},{4,5},{5,4},{6,7},{7,6},{8,9},{9,8},{10,11... | collective-permute-start | bytes 122888 | tf_op jit(solution)/shard_map/ppermute | solution.py:253
  19.3 4.1 %collective-permute-start.8 = (f32[5,8,128]{2,1,0:T(8,128)S(1)}, f32[5,8,128]{2,1,0:T(8,128)S(1)}, u32[]{:S(2)}, u32[]{:S(2)}) collective-permute-start(f32[5,8,128]{2,1,0:T(8,128)S(1)} %slice.4), channel_id=1, source_target_pairs={{0,1},{1,0},{2,3},{3,2},{4,5},{5,4},{6,7},{7,6},{8,9},{9,8},{10,11... | collective-permute-start | bytes 61448 | tf_op jit(solution)/shard_map/ppermute | solution.py:253

commit v5 on v4

--- a/solution.py
+++ b/solution.py
@@ -303,9 +303,8 @@
         name="split_stiffness",
     )(in_hbm(k_cols), in_hbm(k_vals))
 
-    k_split, pair_other, other_late = lax.optimization_barrier((k_split, pair_other, other))
     pair_near = send(pair_other, toward)
-    pair_mine = send(other_late, swap)
+    pair_mine = send(other, swap)
     pieces = [mine, pair_mine, *far]
 
     stiff_shape = (AGG * fine, 256)

time: 24.4 us -> 24.4 us (level)
  starting transfers between devices: 10.8 us -> 12.3 us
  waiting for transfers between devices: 6.73 us -> 5.29 us
    ppermute x9, waiting for transfers between devices: 6.73 us -> 5.29 us  [send(): return lax.ppermute(value, ('row', 'col'), perm)]
    ppermute x9, starting transfers between devices: 10.8 us -> 12.3 us  [send(): return lax.ppermute(value, ('row', 'col'), perm)]
  transfers between devices with their start and end apart: 9 -> 9, of which waited for: 5 -> 4; matrix products, arithmetic and copies ran while one was open for 0% -> 0% of each run, Pallas kernels for 14% -> 14%
where the time goes in v5:
time: 24.4 us; the launch traced here: 24.2 us
  starting transfers between devices  12.3 us (50%)
  Pallas kernels  6.62 us (27%)
  waiting for transfers between devices  5.29 us (22%)
    ppermute x9, starting transfers between devices, send(): return lax.ppermute(value, ('row', 'col'), perm)  12.3 us
    ppermute x9, waiting for transfers between devices, send(): return lax.ppermute(value, ('row', 'col'), perm)  5.29 us
    pallas_call x1, Pallas kernels, body(): pl.pallas_call(functools.partial(split_kernel, slots, total_rows), out_sh...  2.28 us
    pallas_call x1, Pallas kernels, body(): pl.pallas_call(functools.partial(edge_kernel, cols_axis, padded), out_sha...  1.21 us
    pallas_call x1, Pallas kernels, body(): pl.pallas_call(functools.partial(pack_kernel, blocks_all), out_shape=[gro...  1.18 us
    pallas_call x1, Pallas kernels, body(): pl.pallas_call(functools.partial(sum_kernel, padded), out_shape=jax.Shape...  0.86 us
    pallas_call x1, Pallas kernels, body(): pl.pallas_call(stiff_kernel, out_shape=jax.ShapeDtypeStruct(stiff_shape,...  0.55 us
    pallas_call x1, Pallas kernels, body(): pl.pallas_call(functools.partial(inner_kernel, cols_axis, padded), out_sh...  0.55 us
  transfers between devices with their start and end apart: 9, of which 4 were waited for; matrix products, arithmetic and copies ran while one was open for 0% of the time, Pallas kernels for 14%

profile of v5, /device:TPU:0, one launch (start us, length us, event | category | flops | bytes accessed | tf_op | source)
XLA Modules:
  0.0 24.2 jit_solution(5773128060391556447)
XLA Ops:
  0.0 1.2 %pack_window.1 = (f32[4,3,16,128]{3,2,1,0:T(8,128)S(1)}, f32[4,3,16,128]{3,2,1,0:T(8,128)S(1)}, f32[4,3,16,128]{3,2,1,0:T(8,128)S(1)}, f32[4,3,16,128]{3,2,1,0:T(8,128)S(1)}) custom-call(s32[3,16]{1,0:T(4,128)} %bitcast.4, f32[16,3,16,64]{3,2,1,0:T(8,128)} %bitcast.3), custom_call_target="tpu_custom_call" | custom-call | tf_op jit(solution)/shard_map/pack_window/pallas_call | solution.py:269
  1.2 3.1 %collective-permute-start = (f32[4,3,16,128]{3,2,1,0:T(8,128)S(1)}, f32[4,3,16,128]{3,2,1,0:T(8,128)S(1)}, u32[]{:S(2)}, u32[]{:S(2)}) collective-permute-start(f32[4,3,16,128]{3,2,1,0:T(8,128)S(1)} %get-tuple-element.14.refs_0_), channel_id=1, source_target_pairs={{0,1},{1,0},{2,3},{3,2},{4,5},{5,4},{6,7},{7,6},{8,9},{9,8},{10,11... | collective-permute-start | bytes 294920 | tf_op jit(solution)/shard_map/ppermute | solution.py:253
  4.3 2.6 %collective-permute-start.1 = (f32[4,3,16,128]{3,2,1,0:T(8,128)S(1)}, f32[4,3,16,128]{3,2,1,0:T(8,128)S(1)}, u32[]{:S(2)}, u32[]{:S(2)}) collective-permute-start(f32[4,3,16,128]{3,2,1,0:T(8,128)S(1)} %get-tuple-element.15), channel_id=1, source_target_pairs={{0,2},{1,3},{2,0},{3,1},{4,6},{5,7},{6,4},{7,5},{8,10},{9,11},{10,... | collective-permute-start | bytes 294920 | tf_op jit(solution)/shard_map/ppermute | solution.py:253
  6.9 0.0 collective-permute-start.2
  6.9 0.9 %collective-permute-start.5 = (f32[4,3,16,128]{3,2,1,0:T(8,128)S(1)}, f32[4,3,16,128]{3,2,1,0:T(8,128)S(1)}, u32[]{:S(2)}, u32[]{:S(2)}) collective-permute-start(f32[4,3,16,128]{3,2,1,0:T(8,128)S(1)} %get-tuple-element.13.other), channel_id=1, source_target_pairs={{0,1},{1,0},{2,3},{3,2},{4,5},{5,4},{6,7},{7,6},{8,9},{9,8},{10,11... | collective-permute-start | bytes 294920 | tf_op jit(solution)/shard_map/ppermute | solution.py:253
  7.8 0.0 collective-permute-start.3
  7.8 0.0 collective-permute-done.pair_other
  7.8 1.6 %collective-permute-start.4 = (f32[4,3,16,128]{3,2,1,0:T(8,128)S(1)}, f32[4,3,16,128]{3,2,1,0:T(8,128)S(1)}, u32[]{:S(2)}, u32[]{:S(2)}) collective-permute-start(f32[4,3,16,128]{3,2,1,0:T(8,128)S(1)} %collective-permute-done.pair_other), channel_id=1, source_target_pairs={{0,4},{1,29},{2,6},{3,31},{4,8},{5,1},{6,10},{7,3},{8,12},{9,5},{1... | collective-permute-start | bytes 294920 | tf_op jit(solution)/shard_map/ppermute | solution.py:253
  9.4 2.3 %split_stiffness.1.k_ref = bf16[8,25,64,128]{3,2,1,0:T(8,128)(2,1)S(1)} custom-call(s32[16,15]{1,0:T(8,128)} %cols_hbm.1, f32[16,15,64,64]{3,2,1,0:T(8,128)} %k_hbm.1), custom_call_target="tpu_custom_call" | custom-call | bytes 8000000 | tf_op jit(solution)/shard_map/split_stiffness/pallas_call | solution.py:290
  11.7 0.5 %stiff_prolong.1.stiff_other = bf16[512,256]{1,0:T(8,128)(2,1)S(1)} custom-call(f32[4,3,16,128]{3,2,1,0:T(8,128)S(1)} %get-tuple-element.13.other, f32[4,3,16,128]{3,2,1,0:T(8,128)S(1)} %collective-permute-done.pair_other, bf16[8,25,64,128]{3,2,1,0:T(8,128)(2,1)S(1)} %split_stiffness.1.k_ref), custom_call_target="tpu_custom_call" | custom-call | flops 500000000 | bytes 1000000 | tf_op jit(solution)/shard_map/stiff_prolong/pallas_call | solution.py:312
  12.2 2.5 %collective-permute-done.1.refs_1_.refs_2_ = f32[4,3,16,128]{3,2,1,0:T(8,128)S(1)} collective-permute-done((f32[4,3,16,128]{3,2,1,0:T(8,128)S(1)}, f32[4,3,16,128]{3,2,1,0:T(8,128)S(1)}, u32[]{:S(2)}, u32[]{:S(2)}) %collective-permute-start.1) | collective-permute-done | bytes 98336 | tf_op jit(solution)/shard_map/ppermute | solution.py:253
  14.7 0.0 collective-permute-done.2.refs_2_.refs_3_
  14.7 0.0 collective-permute-done.5.refs_5_.refs_1_
  14.7 0.0 collective-permute-done.3.refs_3_
  14.7 0.0 collective-permute-done.4.refs_4_
  14.7 1.2 %edge_terms.1 = (f32[10,8,128]{2,1,0:T(8,128)S(1)}, bf16[2,512,256]{2,1,0:T(8,128)(2,1)S(1)}) custom-call(bf16[8,25,64,128]{3,2,1,0:T(8,128)(2,1)S(1)} %split_stiffness.1.k_ref, bf16[512,256]{1,0:T(8,128)(2,1)S(1)} %stiff_prolong.1.stiff_other, f32[4,3,16,128]{3,2,1,0:T(8,128)S(1)} %get-tuple-element.14.refs_0_, ...), custom_call_target="tpu_custom_call" | custom-call | flops 1000000000 | bytes 2000000 | tf_op jit(solution)/shard_map/edge_terms/pallas_call | solution.py:328
  15.9 1.7 %collective-permute-start.7 = (f32[10,8,128]{2,1,0:T(8,128)S(1)}, f32[10,8,128]{2,1,0:T(8,128)S(1)}, u32[]{:S(2)}, u32[]{:S(2)}) collective-permute-start(f32[10,8,128]{2,1,0:T(8,128)S(1)} %get-tuple-element.20), channel_id=1, source_target_pairs={{0,1},{1,5},{2,3},{3,7},{4,0},{5,9},{6,2},{7,11},{8,4},{9,13},{10,... | collective-permute-start | bytes 122888 | tf_op jit(solution)/shard_map/ppermute | solution.py:253
  17.6 0.5 %inner_terms.1 = (f32[5,16,128]{2,1,0:T(8,128)S(1)}, f32[5,16,128]{2,1,0:T(8,128)S(1)}) custom-call(bf16[512,256]{1,0:T(8,128)(2,1)S(1)} %stiff_prolong.1.stiff_other, bf16[2,512,256]{2,1,0:T(8,128)(2,1)S(1)} %get-tuple-element.17.stiff, f32[4,3,16,128]{3,2,1,0:T(8,128)S(1)} %get-tuple-element.14.refs_0_, ...), custom_call_target="tpu_custom_call" | custom-call | flops 500000000 | bytes 1000000 | tf_op jit(solution)/shard_map/inner_terms/pallas_call | solution.py:346
  18.2 0.1 collective-permute-start.6
  18.2 1.0 %collective-permute-done.7.from_edge = f32[10,8,128]{2,1,0:T(8,128)S(1)} collective-permute-done((f32[10,8,128]{2,1,0:T(8,128)S(1)}, f32[10,8,128]{2,1,0:T(8,128)S(1)}, u32[]{:S(2)}, u32[]{:S(2)}) %collective-permute-start.7) | collective-permute-done | bytes 40992 | tf_op jit(solution)/shard_map/ppermute | solution.py:253
  19.3 2.3 %collective-permute-start.8 = (f32[5,8,128]{2,1,0:T(8,128)S(1)}, f32[5,8,128]{2,1,0:T(8,128)S(1)}, u32[]{:S(2)}, u32[]{:S(2)}) collective-permute-start(f32[5,8,128]{2,1,0:T(8,128)S(1)} %slice.4), channel_id=1, source_target_pairs={{0,1},{1,0},{2,3},{3,2},{4,5},{5,4},{6,7},{7,6},{8,9},{9,8},{10,11... | collective-permute-start | bytes 61448 | tf_op jit(solution)/shard_map/ppermute | solution.py:253
  21.6 0.8 %collective-permute-done.6.from_pair = f32[5,16,128]{2,1,0:T(8,128)S(1)} collective-permute-done((f32[5,16,128]{2,1,0:T(8,128)S(1)}, f32[5,16,128]{2,1,0:T(8,128)S(1)}, u32[]{:S(2)}, u32[]{:S(2)}) %collective-permute-start.6) | collective-permute-done | bytes 40992 | tf_op jit(solution)/shard_map/ppermute | solution.py:253
  22.4 1.0 %collective-permute-done.8.from_pair_edge = f32[5,8,128]{2,1,0:T(8,128)S(1)} collective-permute-done((f32[5,8,128]{2,1,0:T(8,128)S(1)}, f32[5,8,128]{2,1,0:T(8,128)S(1)}, u32[]{:S(2)}, u32[]{:S(2)}) %collective-permute-start.8) | collective-permute-done | bytes 20512 | tf_op jit(solution)/shard_map/ppermute | solution.py:253
  23.4 0.9 %sum_terms.1 = f32[2,7,16,64]{3,2,1,0:T(8,128)} custom-call(f32[5,16,128]{2,1,0:T(8,128)S(1)} %get-tuple-element.18.own, f32[5,16,128]{2,1,0:T(8,128)S(1)} %collective-permute-done.6.from_pair, f32[10,8,128]{2,1,0:T(8,128)S(1)} %collective-permute-done.7.from_edge, f32[5,8,128]{2,1,0:T(8,128)S(1)} %collective-permute-done.8.from_pair_edge), custom_call_target="tpu_custom_call" | custom-call | tf_op jit(solution)/shard_map/sum_terms/pallas_call | solution.py:361
  (1 shorter events, 0.0 us)
Async XLA Ops:
  1.2 6.6 %collective-permute-start = (f32[4,3,16,128]{3,2,1,0:T(8,128)S(1)}, f32[4,3,16,128]{3,2,1,0:T(8,128)S(1)}, u32[]{:S(2)}, u32[]{:S(2)}) collective-permute-start(f32[4,3,16,128]{3,2,1,0:T(8,128)S(1)} %get-tuple-element.14.refs_0_), channel_id=1, source_target_pairs={{0,1},{1,0},{2,3},{3,2},{4,5},{5,4},{6,7},{7,6},{8,9},{9,8},{10,11... | collective-permute-start | bytes 294920 | tf_op jit(solution)/shard_map/ppermute | solution.py:253
  4.3 10.4 %collective-permute-start.1 = (f32[4,3,16,128]{3,2,1,0:T(8,128)S(1)}, f32[4,3,16,128]{3,2,1,0:T(8,128)S(1)}, u32[]{:S(2)}, u32[]{:S(2)}) collective-permute-start(f32[4,3,16,128]{3,2,1,0:T(8,128)S(1)} %get-tuple-element.15), channel_id=1, source_target_pairs={{0,2},{1,3},{2,0},{3,1},{4,6},{5,7},{6,4},{7,5},{8,10},{9,11},{10,... | collective-permute-start | bytes 294920 | tf_op jit(solution)/shard_map/ppermute | solution.py:253
  6.9 7.8 %collective-permute-start.2 = (f32[4,3,16,128]{3,2,1,0:T(8,128)S(1)}, f32[4,3,16,128]{3,2,1,0:T(8,128)S(1)}, u32[]{:S(2)}, u32[]{:S(2)}) collective-permute-start(f32[4,3,16,128]{3,2,1,0:T(8,128)S(1)} %get-tuple-element.16), channel_id=1, source_target_pairs={{0,3},{1,2},{2,1},{3,0},{4,7},{5,6},{6,5},{7,4},{8,11},{9,10},{10,... | collective-permute-start | bytes 294920 | tf_op jit(solution)/shard_map/ppermute | solution.py:253
  6.9 7.8 %collective-permute-start.5 = (f32[4,3,16,128]{3,2,1,0:T(8,128)S(1)}, f32[4,3,16,128]{3,2,1,0:T(8,128)S(1)}, u32[]{:S(2)}, u32[]{:S(2)}) collective-permute-start(f32[4,3,16,128]{3,2,1,0:T(8,128)S(1)} %get-tuple-element.13.other), channel_id=1, source_target_pairs={{0,1},{1,0},{2,3},{3,2},{4,5},{5,4},{6,7},{7,6},{8,9},{9,8},{10,11... | collective-permute-start | bytes 294920 | tf_op jit(solution)/shard_map/ppermute | solution.py:253
  7.8 6.9 %collective-permute-start.3 = (f32[4,3,16,128]{3,2,1,0:T(8,128)S(1)}, f32[4,3,16,128]{3,2,1,0:T(8,128)S(1)}, u32[]{:S(2)}, u32[]{:S(2)}) collective-permute-start(f32[4,3,16,128]{3,2,1,0:T(8,128)S(1)} %get-tuple-element.13.other), channel_id=1, source_target_pairs={{0,4},{1,29},{2,6},{3,31},{4,8},{5,1},{6,10},{7,3},{8,12},{9,5},{1... | collective-permute-start | bytes 294920 | tf_op jit(solution)/shard_map/ppermute | solution.py:253
  7.8 6.9 %collective-permute-start.4 = (f32[4,3,16,128]{3,2,1,0:T(8,128)S(1)}, f32[4,3,16,128]{3,2,1,0:T(8,128)S(1)}, u32[]{:S(2)}, u32[]{:S(2)}) collective-permute-start(f32[4,3,16,128]{3,2,1,0:T(8,128)S(1)} %collective-permute-done.pair_other), channel_id=1, source_target_pairs={{0,4},{1,29},{2,6},{3,31},{4,8},{5,1},{6,10},{7,3},{8,12},{9,5},{1... | collective-permute-start | bytes 294920 | tf_op jit(solution)/shard_map/ppermute | solution.py:253
  15.9 3.3 %collective-permute-start.7 = (f32[10,8,128]{2,1,0:T(8,128)S(1)}, f32[10,8,128]{2,1,0:T(8,128)S(1)}, u32[]{:S(2)}, u32[]{:S(2)}) collective-permute-start(f32[10,8,128]{2,1,0:T(8,128)S(1)} %get-tuple-element.20), channel_id=1, source_target_pairs={{0,1},{1,5},{2,3},{3,7},{4,0},{5,9},{6,2},{7,11},{8,4},{9,13},{10,... | collective-permute-start | bytes 122888 | tf_op jit(solution)/shard_map/ppermute | solution.py:253
  18.2 4.2 %collective-permute-start.6 = (f32[5,16,128]{2,1,0:T(8,128)S(1)}, f32[5,16,128]{2,1,0:T(8,128)S(1)}, u32[]{:S(2)}, u32[]{:S(2)}) collective-permute-start(f32[5,16,128]{2,1,0:T(8,128)S(1)} %get-tuple-element.19), channel_id=1, source_target_pairs={{0,1},{1,0},{2,3},{3,2},{4,5},{5,4},{6,7},{7,6},{8,9},{9,8},{10,11... | collective-permute-start | bytes 122888 | tf_op jit(solution)/shard_map/ppermute | solution.py:253
  19.3 4.1 %collective-permute-start.8 = (f32[5,8,128]{2,1,0:T(8,128)S(1)}, f32[5,8,128]{2,1,0:T(8,128)S(1)}, u32[]{:S(2)}, u32[]{:S(2)}) collective-permute-start(f32[5,8,128]{2,1,0:T(8,128)S(1)} %slice.4), channel_id=1, source_target_pairs={{0,1},{1,0},{2,3},{3,2},{4,5},{5,4},{6,7},{7,6},{8,9},{9,8},{10,11... | collective-permute-start | bytes 61448 | tf_op jit(solution)/shard_map/ppermute | solution.py:253
